TPU v7x, 256 devices: a whole 4x4x8 slice. The times are simulated.
256 devices in a mesh: rep: 4 (over y), shard: 64 (over x, z, core).
Axes of the slice: x: 4, y: 4, z: 8, core: 2. Of those that a mesh axis runs over, the one named last changes fastest.
Arguments:
- grad: bfloat16 [48, 1024, 1024], P(None, 'shard', 'rep'), may hold values from -2 to 2
- first_moment: float32 [48, 1024, 1024], P(None, 'shard', 'rep'), may hold values from -2 to 2
- second_moment: float32 [48, 1024, 1024], P(None, 'shard', 'rep'), may hold values from 0.0001 to 0.001
- stat_left: float32 [64, 1024, 1024], P('shard', 'rep'), may hold values from -1 to 3
- stat_right: float32 [64, 1024, 1024], P('shard', 'rep'), may hold values from -1 to 3
- root_left: bfloat16 [64, 1024, 1024], P('shard', 'rep'), may hold values from -1 to 3
- root_right: bfloat16 [64, 1024, 1024], P('shard', None, 'rep'), may hold values from -1 to 3
- owner_slot: int32 [48], replicated, may hold values from 0 to 63, as said below
Outputs:
- update: bfloat16 [48, 1024, 1024], P(None, 'shard', 'rep')
- new_first: float32 [48, 1024, 1024], P(None, 'shard', 'rep')
- new_second: float32 [48, 1024, 1024], P(None, 'shard', 'rep')
- new_left: float32 [64, 1024, 1024], P('shard', 'rep')
- new_right: float32 [64, 1024, 1024], P('shard', 'rep')
Inputs may be any that keep to these rules, and one draw needn't show every extreme that they name: `owner_slot`: no two blocks share a value; each device along `shard` holds one slot, and the block whose value is o is owned by device o along `shard`. Owners without a block hold slots that no block names.
All inputs are finite; a program needn't handle non-finite values.
Results may differ from a plain program's by a relative error of at most 0.012.
Values may be sent and summed in bfloat16 or wider, within the bound.
A program may use at most 64 MiB of HBM per device.

v0:
```python
import jax
import jax.numpy as jnp
from jax import lax
from jax.sharding import PartitionSpec as P

beta_one = 0.9
beta_two = 0.95
adam_eps = 1e-08
norm_eps = 1e-06


def per_device(
    grad, first_moment, second_moment, stat_left, stat_right, root_left, root_right, owner_slot
):
    shard_count = lax.axis_size("shard")
    group_rank = lax.axis_index("rep")
    block_count, row_count, col_count = grad.shape
    slot_count = stat_left.shape[0]
    own_span = stat_left.shape[1]
    full_width = row_count * shard_count
    slot_table = (
        jnp.arange(shard_count, dtype=jnp.int32)[None, :] * slot_count
        + jnp.arange(slot_count, dtype=jnp.int32)[:, None]
    )
    selector = (owner_slot[None, None, :] == slot_table[:, :, None]).astype(jnp.bfloat16)
    outgoing = jnp.einsum(
        "cob,brk->cork", selector, grad, preferred_element_type=jnp.float32
    ).astype(jnp.bfloat16)
    incoming = lax.all_to_all(outgoing, "shard", split_axis=1, concat_axis=2, tiled=True)
    column_piece = incoming.reshape(slot_count, full_width, col_count)
    matrices = lax.all_gather(column_piece, "rep", axis=2, tiled=True)
    own_rows = lax.dynamic_slice_in_dim(matrices, group_rank * own_span, own_span, 1)
    own_cols = lax.dynamic_slice_in_dim(matrices, group_rank * own_span, own_span, 2)
    new_left = stat_left + jnp.einsum(
        "cik,cjk->cij", own_rows, matrices, preferred_element_type=jnp.float32
    )
    new_right = stat_right + jnp.einsum(
        "cki,ckj->cij", own_cols, matrices, preferred_element_type=jnp.float32
    )
    left_part = jnp.einsum("cik,ckj->cij", root_left, matrices, preferred_element_type=jnp.float32)
    right_wide = root_right.astype(jnp.float32)
    precond = jnp.einsum(
        "cij,cjk->cik",
        lax.all_gather(left_part, "rep", axis=1, tiled=True),
        right_wide,
        preferred_element_type=jnp.float32,
    )
    precond = precond.astype(jnp.bfloat16)
    outbound = precond.reshape(slot_count, shard_count, row_count, col_count)
    returned = lax.all_to_all(outbound, "shard", split_axis=1, concat_axis=1, tiled=True)
    pieces = jnp.einsum("cob,cork->brk", selector, returned, preferred_element_type=jnp.float32)
    grad_wide = grad.astype(jnp.float32)
    new_first = beta_one * first_moment + (1.0 - beta_one) * grad_wide
    new_second = beta_two * second_moment + (1.0 - beta_two) * grad_wide * grad_wide
    adam = new_first / (jnp.sqrt(new_second) + adam_eps)
    adam_sq, precond_sq = lax.psum(
        (jnp.sum(adam * adam, axis=(1, 2)), jnp.sum(pieces * pieces, axis=(1, 2))), ("rep", "shard")
    )
    factor = jnp.sqrt(adam_sq) / (jnp.sqrt(precond_sq) + norm_eps)
    update = (-factor[:, None, None] * pieces).astype(jnp.bfloat16)
    return (update, new_first, new_second, new_left, new_right)


def solution(mesh):
    placed = (
        P(None, "shard", "rep"),
        P(None, "shard", "rep"),
        P(None, "shard", "rep"),
        P("shard", "rep", None),
        P("shard", "rep", None),
        P("shard", "rep", None),
        P("shard", None, "rep"),
        P(),
    )
    return jax.shard_map(
        per_device,
        mesh=mesh,
        in_specs=placed,
        out_specs=(
            P(None, "shard", "rep"),
            P(None, "shard", "rep"),
            P(None, "shard", "rep"),
            P("shard", "rep", None),
            P("shard", "rep", None),
        ),
        check_vma=False,
    )
```

profile of v0, /device:TPU:1, one launch (start us, length us, event | category | flops | bytes accessed | tf_op | source)
XLA Modules:
  0.0 229.6 jit_solution(4488412409465390527)
XLA Ops:
  7.2 0.0 copy-start
  7.2 0.0 all-gather.4.cloned.1.call-start
  7.2 1.5 fusion.21
  8.7 0.3 copy.21
  9.0 30.2 %all_to_all.14 = bf16[1,64,16,256]{3,2,0,1:T(8,128)(2,1)} all-to-all(bf16[1,64,16,256]{3,2,0,1:T(8,128)(2,1)S(1)} %copy.21), channel_id=1, replica_groups=mesh['rep'=4,'shard'=64] {'shard'}, dimensions={1} | all-to-all | bytes 1048576 | tf_op jit(solution)/shard_map/all_to_all | solution.py:29
  39.2 0.0 all-gather.4.cloned.1.call-update
  39.2 0.0 copy-start.6
  39.3 0.0 all-gather.6.cloned.1.call-start
  39.3 33.4 %all-gather.4.cloned.1.call-done = bf16[1,1024,1024]{2,1,0:T(8,128)(2,1)} async-done(((bf16[1,1024,256]{2,1,0:T(8,128)(2,1)}), bf16[1,1024,1024]{2,1,0:T(8,128)(2,1)}) %all-gather.4.cloned.1.call-update) | async-done | bytes 2097168 | tf_op jit(solution)/shard_map/all_gather | solution.py:31
  72.7 0.0 copy-done
  72.7 3.2 %fusion.6 = bf16[256,1024]{0,1:T(8,128)(2,1)} fusion(bf16[1,1024,1024]{2,1,0:T(8,128)(2,1)} %all-gather.4.cloned.1.call-done, bf16[1,256,1024]{2,1,0:T(8,128)(2,1)S(1)} %copy-done), kind=kOutput, calls=%fused_computation.6 | convolution fusion | flops 536870912 | bytes 3145728 | tf_op jit(solution)/shard_map/cik,ckj->cij/dot_general | solution.py:40
  75.9 0.0 all-gather.6.cloned.1.call-update
  75.9 0.0 copy-start.2
  75.9 38.2 %all-gather.6.cloned.1.call-done = bf16[1024,1024]{0,1:T(8,128)(2,1)} async-done(((bf16[256,1024]{0,1:T(8,128)(2,1)}), bf16[1024,1024]{0,1:T(8,128)(2,1)}) %all-gather.6.cloned.1.call-update) | async-done | bytes 2097168 | tf_op jit(solution)/shard_map/all_gather | solution.py:44
  114.1 0.0 copy-done.6
  114.1 3.2 %convolution_convert_fusion = bf16[1024,256]{1,0:T(8,128)(2,1)} fusion(bf16[1024,1024]{0,1:T(8,128)(2,1)} %all-gather.6.cloned.1.call-done, bf16[1,1024,256]{2,1,0:T(8,128)(2,1)S(1)} %copy-done.6), kind=kOutput, calls=%fused_computation.11 | convolution fusion | flops 536870912 | bytes 3145728 | tf_op jit(solution)/shard_map/cij,cjk->cik/dot_general | solution.py:42
  117.3 0.0 copy-start.1
  117.3 11.7 %all-to-all-start.1 = ((bf16[1,64,16,256]{3,2,0,1:T(8,128)(2,1)}), bf16[1,64,16,256]{3,2,0,1:T(8,128)(2,1)S(1)}, u32[]{:S(2)}, u32[]{:S(2)}) async-start(bf16[1,64,16,256]{3,2,0,1:T(8,128)(2,1)} %bitcast.58), calls=%async_computation.1 | async-start | bytes 1048576 | tf_op jit(solution)/shard_map/all_to_all | solution.py:50
  128.9 0.0 copy-done.2
  128.9 0.0 copy-start.3
  128.9 3.2 %multiply_reduce_fusion.1 = (f32[48]{0:T(128)S(1)}, f32[48,16,256]{2,1,0:T(8,128)}, f32[48,16,256]{2,1,0:T(8,128)}) fusion(bf16[48,16,256]{2,1,0:T(8,128)(2,1)S(1)} %copy-done.2, f32[48,16,256]{2,1,0:T(8,128)} %param.10, f32[48,16,256]{2,1,0:T(8,128)} %param.9), kind=kLoop, calls=%fused_computation.20 | loop fusion | flops 2359248 | bytes 3539136 | tf_op jit(solution)/shard_map/reduce_sum | solution.py:57
  132.1 0.0 copy-done.1
  132.1 0.0 copy-done.3
  132.1 0.0 copy-start.4
  132.1 1.7 fusion.18
  133.9 0.0 copy-done.4
  133.9 0.0 copy-start.5
  133.9 1.7 fusion.15
  135.6 10.6 %all-to-all-done.1 = bf16[1,64,16,256]{3,2,0,1:T(8,128)(2,1)S(1)} async-done(((bf16[1,64,16,256]{3,2,0,1:T(8,128)(2,1)}), bf16[1,64,16,256]{3,2,0,1:T(8,128)(2,1)S(1)}, u32[]{:S(2)}, u32[]{:S(2)}) %all-to-all-start.1) | async-done | bytes 524320 | tf_op jit(solution)/shard_map/all_to_all | solution.py:50
  146.2 0.0 copy-done.5
  146.2 0.4 multiply_reduce_fusion
  146.7 75.1 %all-reduce = (f32[48]{0:T(128)S(1)}, f32[48]{0:T(128)S(1)}) all-reduce(f32[48]{0:T(128)S(1)} %get-tuple-element.25, f32[48]{0:T(128)S(1)} %get-tuple-element.22), channel_id=1, replica_groups=mesh['rep'=4,'shard'=64] {'rep','shard'}, use_global_device_ids=true, to_apply=%region_3.0 | all-reduce | flops 96 | bytes 768 | tf_op jit(solution)/shard_map/psum | solution.py:56
  221.7 0.1 multiply_convert_fusion
  221.9 0.9 copy.24
  (1 shorter events, 0.0 us)
Async XLA Ops:
  7.2 65.5 %copy-start = (bf16[1,256,1024]{2,1,0:T(8,128)(2,1)S(1)}, bf16[1,256,1024]{2,1,0:T(8,128)(2,1)}, u32[]{:S(2)}) copy-start(bf16[1,256,1024]{2,1,0:T(8,128)(2,1)} %param.13) | copy-start | bytes 1572868
  7.2 65.5 %all-gather.4.cloned.1.call-start = ((), (), s32[]{:S(2)}) async-start(), calls=%async_computation.2 | async-start | bytes 2621440 | tf_op jit(solution)/shard_map/all_gather | solution.py:31
  39.2 74.8 %copy-start.6 = (bf16[1,1024,256]{2,1,0:T(8,128)(2,1)S(1)}, bf16[1,1024,256]{2,1,0:T(8,128)(2,1)}, u32[]{:S(2)}) copy-start(bf16[1,1024,256]{2,1,0:T(8,128)(2,1)} %param.14) | copy-start | bytes 1572868
  39.3 74.8 %all-gather.6.cloned.1.call-start = ((), (), s32[]{:S(2)}) async-start(), calls=%async_computation.3 | async-start | bytes 2621440 | tf_op jit(solution)/shard_map/all_gather | solution.py:44
  75.9 53.0 %copy-start.2 = (bf16[48,16,256]{2,1,0:T(8,128)(2,1)S(1)}, bf16[48,16,256]{2,1,0:T(8,128)(2,1)}, u32[]{:S(2)}) copy-start(bf16[48,16,256]{2,1,0:T(8,128)(2,1)} %param.8) | copy-start | bytes 1179652
  117.3 14.9 %copy-start.1 = (bf16[1,1024,1024]{2,1,0:T(8,128)(2,1)S(1)}, bf16[1,1024,1024]{2,1,0:T(8,128)(2,1)}, u32[]{:S(2)}) copy-start(bf16[1,1024,1024]{2,1,0:T(8,128)(2,1)} %all-gather.4.cloned.1.call-done) | copy-start | bytes 6291460
  117.3 29.0 %all-to-all-start.1 = ((bf16[1,64,16,256]{3,2,0,1:T(8,128)(2,1)}), bf16[1,64,16,256]{3,2,0,1:T(8,128)(2,1)S(1)}, u32[]{:S(2)}, u32[]{:S(2)}) async-start(bf16[1,64,16,256]{3,2,0,1:T(8,128)(2,1)} %bitcast.58), calls=%async_computation.1 | async-start | bytes 1048576 | tf_op jit(solution)/shard_map/all_to_all | solution.py:50
  128.9 3.2 %copy-start.3 = (f32[1,256,1024]{2,1,0:T(8,128)S(1)}, f32[1,256,1024]{2,1,0:T(8,128)}, u32[]{:S(2)}) copy-start(f32[1,256,1024]{2,1,0:T(8,128)} %param.11) | copy-start | bytes 3145732
  132.1 1.7 copy-start.4
  133.9 12.4 %copy-start.5 = (s32[48]{0:T(128)S(1)}, s32[48]{0:T(128)}, u32[]{:S(2)}) copy-start(s32[48]{0:T(128)} %param.15) | copy-start | bytes 580
Sparse Core Ops, SparseCore 0:
  39.4 33.2 all-gather.3
  76.0 38.0 all-gather.5
where the time goes:
time: 230 us
  blocking collectives  105 us (46%)
  waiting for transfers between devices  82.3 us (36%)
  between operations  14.1 us (6%)
  starting transfers between devices  11.7 us (5%)
  matrix products  11.7 us (5%)
  other arithmetic  3.32 us (1%)
    psum x1, blocking collectives, per_device(): lax.psum((jnp.sum(adam * adam, axis=(1, 2)), jnp.sum(pieces * pieces, axi...  75.1 us
    all_gather x1, waiting for transfers between devices, per_device(): lax.all_gather(left_part, 'rep', axis=1, tiled=True)  38.2 us
    all_gather x1, waiting for transfers between devices, per_device(): matrices = lax.all_gather(column_piece, 'rep', axis=2, tiled=True)  33.4 us
    all_to_all x1, blocking collectives, per_device(): lax.all_to_all(outgoing, 'shard', split_axis=1, concat_axis=2, tiled=True)  30.2 us
    all_to_all x1, starting transfers between devices, per_device(): lax.all_to_all(outbound, 'shard', split_axis=1, concat_axis=1, tiled=True)  11.7 us
    all_to_all x1, waiting for transfers between devices, per_device(): lax.all_to_all(outbound, 'shard', split_axis=1, concat_axis=1, tiled=True)  10.6 us
  transfers between devices with their start and end apart: 3, of which 3 were waited for; matrix products, arithmetic and copies ran while one was open for 3% of the time, Pallas kernels for 0%

commit v1 on v0

v1 whole, which is shorter than its diff:
```python
import functools

import jax
import jax.numpy as jnp
from jax import lax
from jax.experimental import pallas as pl
from jax.experimental.pallas import tpu as pltpu
from jax.sharding import PartitionSpec as P

beta_one = 0.9
beta_two = 0.95
adam_eps = 1e-08
norm_eps = 1e-06

MESH = pl.DeviceIdType.MESH
f32 = jnp.float32
bf16 = jnp.bfloat16

NX, NZ, NC, NY = 4, 8, 2, 4
NS = NX * NZ * NC
GROUP = NZ * NC
X_ORDER = (0, 1, 3, 2)


def remote(src, dst, send_sem, recv_sem, device):
    return pltpu.make_async_remote_copy(
        src_ref=src,
        dst_ref=dst,
        send_sem=send_sem,
        recv_sem=recv_sem,
        device_id=device,
        device_id_type=MESH,
    )


def await_bytes(ref, sem):
    pltpu.make_async_copy(ref, ref, sem).wait()


def rows_of(index, count):
    return pl.ds(pl.multiple_of(index * count, count), count)


class ColumnGather:
    def __init__(self, buf, rows, sems, r, s):
        self.buf, self.rows = buf, rows
        self.own_send, self.own_recv, self.fwd_send, self.fwd_recv = sems
        self.r, self.s = r, s
        self.up = lax.rem(r + 1, NY)
        self.down = lax.rem(r + NY - 1, NY)
        self.opposite = lax.rem(r + 2, NY)

    def own(self, k, way):
        ref = self.buf.at[self.r, self.rows[k]]
        target = (self.up, self.down)[way]
        return remote(ref, ref, self.own_send.at[way, k], self.own_recv.at[way, k], (target, self.s))

    def arrived(self, k, way):
        ref = self.buf.at[(self.down, self.up)[way], self.rows[k]]
        await_bytes(ref, self.own_recv.at[way, k])

    def forward(self, k):
        way = k % 2
        ref = self.buf.at[(self.down, self.up)[way], self.rows[k]]
        target = (self.up, self.down)[way]
        return remote(ref, ref, self.fwd_send.at[k], self.fwd_recv.at[k], (target, self.s))

    def send(self, k):
        self.own(k, 0).start()
        self.own(k, 1).start()

    def pass_on(self, k):
        self.arrived(k, 0)
        self.arrived(k, 1)
        self.forward(k).start()

    def last(self, k):
        ref = self.buf.at[self.opposite, self.rows[k]]
        await_bytes(ref, self.fwd_recv.at[k])

    def drain(self):
        for k in range(4):
            self.own(k, 0).wait_send()
            self.own(k, 1).wait_send()
            self.forward(k).wait_send()


class SmallSum:
    def __init__(self, buf, send_sem, recv_sem, r, s):
        self.buf, self.send_sem, self.recv_sem = buf, send_sem, recv_sem
        x, z, c = lax.div(s, GROUP), lax.rem(lax.div(s, NC), NZ), lax.rem(s, NC)
        self.stages = {
            "core": (0, NC, c, lambda p: (r, s - c + p)),
            "z": (NC, NZ, z, lambda p: (r, (x * NZ + p) * NC + c)),
            "x": (NC + NZ, NX, x, lambda p: (r, p * GROUP + lax.rem(s, GROUP))),
            "y": (NC + NZ + NX, NY, r, lambda p: (p, s)),
        }

    def start(self, stage, tile):
        base, count, me, where = self.stages[stage]
        number = tuple(self.stages).index(stage)
        self.buf[base + me] = tile
        for step in range(1, count):
            p = lax.rem(me + step, count)
            ref = self.buf.at[base + me]
            remote(ref, ref, self.send_sem.at[number], self.recv_sem.at[number], where(p)).start()

    def finish(self, stage):
        base, count, me, where = self.stages[stage]
        number = tuple(self.stages).index(stage)
        others = self.buf.at[pl.ds(base, count - 1)]
        await_bytes(others, self.recv_sem.at[number])
        await_bytes(others, self.send_sem.at[number])
        total = self.buf[base]
        for p in range(1, count):
            total = total + self.buf[base + p]
        return total


SMALL = NC + NZ + NX + NY


def kernel(
    owner, inv, grad, m1, m2, stat_l, stat_r, root_l, root_r,
    update_out, first_out, second_out, left_out, right_out,
    gv, m1v, m2v, slv, srv, rlf, rrv, outb, gc, tv, pv, rc2, upv, acc, small_a, small_p,
    in_sem, out_sem, bulk_send, bulk_recv, back_send, back_recv,
    g_os, g_or, g_fs, g_fr, l_os, l_or, l_fs, l_fr,
    sa_send, sa_recv, sp_send, sp_recv,
):
    r = lax.axis_index("rep")
    s = lax.axis_index("shard")
    x = lax.div(s, GROUP)
    zc = lax.rem(s, GROUP)
    nblk = gv.shape[0]

    def load(i, src, dst):
        return pltpu.make_async_copy(src, dst, in_sem.at[i])

    loads = (
        load(0, grad, gv),
        load(1, root_l, rlf.at[r]),
        load(2, m1, m1v),
        load(3, m2, m2v),
        load(4, root_r, rrv),
        load(5, stat_l, slv),
        load(6, stat_r, srv),
    )
    for copy in loads:
        copy.start()

    barrier = pltpu.get_barrier_semaphore()

    def greet(i, carry):
        pl.semaphore_signal(
            barrier, inc=1, device_id=(r, lax.rem(s + i, NS)), device_id_type=MESH
        )
        return carry

    lax.fori_loop(1, NS, greet, 0)
    for step in range(1, NY):
        pl.semaphore_signal(
            barrier, inc=1, device_id=(lax.rem(r + step, NY), s), device_id_type=MESH
        )

    loads[0].wait()

    def pick(slot, carry):
        outb[slot] = gv[jnp.maximum(inv[slot], 0)]
        return carry

    lax.fori_loop(0, NS, pick, 0, unroll=4)
    loads[1].wait()
    pl.semaphore_wait(barrier, NS - 1 + NY - 1)

    mine = gc.at[r, rows_of(s, 16)]
    pltpu.make_async_copy(outb.at[s], mine, bulk_recv.at[x]).start()

    def send_rows(dx):
        plane = lax.rem(x + dx, NX)

        def body(i, carry):
            peer = plane * GROUP + lax.rem(zc + i, GROUP)
            remote(outb.at[peer], mine, bulk_send, bulk_recv.at[x], (r, peer)).start()
            return carry

        lax.fori_loop(1 if dx == 0 else 0, GROUP, body, 0)

    quarter = GROUP * 16
    grads = ColumnGather(
        gc,
        [rows_of(lax.rem(x + NX - dx, NX), quarter) for dx in X_ORDER],
        (g_os, g_or, g_fs, g_fr), r, s,
    )
    lefts = ColumnGather(rlf, [pl.ds(64 * k, 64) for k in range(4)], (l_os, l_or, l_fs, l_fr), r, s)

    send_rows(X_ORDER[0])
    for k in range(4):
        lefts.send(k)
    for dx in X_ORDER[1:]:
        send_rows(dx)

    loads[2].wait()
    loads[3].wait()

    def adam(b, carry):
        g = gv[b].astype(f32)
        first = beta_one * m1v[b] + (1.0 - beta_one) * g
        second = beta_two * m2v[b] + (1.0 - beta_two) * g * g
        m1v[b] = first
        m2v[b] = second
        step = first / (jnp.sqrt(second) + adam_eps)
        step = step * step
        step = step[:, :128] + step[:, 128:]
        acc[pl.ds(b, 1), :] = jnp.sum(step, axis=0, keepdims=True)
        return carry

    lax.fori_loop(0, nblk, adam, 0, unroll=2)
    store_first = pltpu.make_async_copy(m1v, first_out, out_sem.at[0])
    store_second = pltpu.make_async_copy(m2v, second_out, out_sem.at[1])
    store_first.start()
    store_second.start()
    sums = jnp.sum(acc[...], axis=1, keepdims=True)
    lane = lax.broadcasted_iota(jnp.int32, (nblk, 128), 1)
    row = lax.broadcasted_iota(jnp.int32, (nblk, 128), 0)
    vec = jnp.sum(jnp.where(lane == row, sums, 0.0), axis=0, keepdims=True)
    vec = jnp.broadcast_to(vec, (8, 128))
    adam_sum = SmallSum(small_a, sa_send, sa_recv, r, s)
    adam_sum.start("core", vec)

    def group_in(k):
        plane = lax.rem(x + NX - X_ORDER[k], NX)
        await_bytes(gc.at[r, rows_of(plane, quarter)], bulk_recv.at[plane])

    group_in(0)
    grads.send(0)
    adam_sum.start("z", adam_sum.finish("core"))
    lefts.pass_on(0)
    lefts.pass_on(1)
    group_in(1)
    grads.send(1)
    adam_sum.start("x", adam_sum.finish("z"))
    lefts.pass_on(2)
    group_in(2)
    grads.send(2)
    lefts.pass_on(3)
    group_in(3)
    grads.send(3)
    adam_sum.start("y", adam_sum.finish("x"))
    for k in range(4):
        grads.pass_on(k)
    adam_sq = adam_sum.finish("y")
    for k in range(4):
        lefts.last(k)
    for k in range(4):
        grads.last(k)

    loads[4].wait()

    def right_rows(m, carry):
        rows = rows_of(m, 256)
        total = jnp.zeros((256, 256), f32)
        for q in range(NY):
            total += jnp.dot(gc[q, rows, :], rrv[pl.ds(256 * q, 256), :], preferred_element_type=f32)
        tv[rows, :] = total.astype(bf16)
        return carry

    lax.fori_loop(0, 4, right_rows, 0)

    def left_rows(m, total):
        part = jnp.dot(rlf[m], tv[...], preferred_element_type=f32).astype(bf16)
        pv[rows_of(m, 256), :] = part
        wide = part.astype(f32)
        return total + jnp.sum(wide * wide, axis=0, keepdims=True)

    norm = lax.fori_loop(0, 4, left_rows, jnp.zeros((1, 256), f32))
    norm = jnp.sum(norm, axis=1, keepdims=True)
    block = inv[s]
    lanes = lax.broadcasted_iota(jnp.int32, (8, 128), 1)
    spot = jnp.where(lanes == block, jnp.broadcast_to(norm, (8, 128)), 0.0)
    norm_sum = SmallSum(small_p, sp_send, sp_recv, r, s)
    norm_sum.start("y", spot)

    pltpu.make_async_copy(pv.at[rows_of(s, 16)], rc2.at[s], back_recv).start()
    for dx in X_ORDER[::-1]:
        plane = lax.rem(x + dx, NX)

        def body(i, carry, plane=plane):
            peer = plane * GROUP + lax.rem(zc + i, GROUP)
            remote(pv.at[rows_of(peer, 16)], rc2.at[s], back_send, back_recv, (r, peer)).start()
            return carry

        lax.fori_loop(1 if dx == 0 else 0, GROUP, body, 0)

    has = (block >= 0).astype(f32)
    loads[5].wait()
    loads[6].wait()
    norm_sum.start("core", norm_sum.finish("y"))

    def gram_left(j, carry):
        cols = rows_of(j, 256)
        total = jnp.zeros((256, 256), f32)
        for q in range(NY):
            total += lax.dot_general(
                gc[q, rows_of(r, 256), :], gc[q, cols, :], (((1,), (1,)), ((), ())),
                preferred_element_type=f32,
            )
        slv[:, cols] = slv[:, cols] + has * total
        return carry

    lax.fori_loop(0, 4, gram_left, 0)
    store_left = pltpu.make_async_copy(slv, left_out, out_sem.at[2])
    store_left.start()
    norm_sum.start("z", norm_sum.finish("core"))

    def gram_right(q, carry):
        cols = rows_of(q, 256)
        total = lax.dot_general(
            gc[r], gc[q], (((0,), (0,)), ((), ())), preferred_element_type=f32
        )
        srv[:, cols] = srv[:, cols] + has * total
        return carry

    lax.fori_loop(0, 4, gram_right, 0)
    store_right = pltpu.make_async_copy(srv, right_out, out_sem.at[3])
    store_right.start()
    norm_sum.start("x", norm_sum.finish("z"))
    norm_sq = norm_sum.finish("x")

    factor = -(jnp.sqrt(adam_sq) / (jnp.sqrt(norm_sq) + norm_eps))
    await_bytes(rc2, back_recv)
    for b in range(nblk):
        scale = jnp.broadcast_to(factor[0:1, b : b + 1], (16, 256))
        upv[b] = (scale * rc2[owner[b]].astype(f32)).astype(bf16)
    store_update = pltpu.make_async_copy(upv, update_out, out_sem.at[4])
    store_update.start()

    grads.drain()
    lefts.drain()
    sent = gc.at[0, pl.ds(0, (NS - 1) * 16)]
    await_bytes(sent, bulk_send)
    await_bytes(sent, back_send)
    store_first.wait()
    store_second.wait()
    store_left.wait()
    store_right.wait()
    store_update.wait()


def per_device(
    grad, first_moment, second_moment, stat_left, stat_right, root_left, root_right, owner_slot
):
    slots = jnp.arange(NS, dtype=jnp.int32)
    numbers = jnp.arange(1, owner_slot.shape[0] + 1, dtype=jnp.int32)
    inverse = jnp.sum(
        jnp.where(owner_slot[None, :] == slots[:, None], numbers[None, :], 0), axis=1
    ) - 1
    nblk, rows, cols = grad.shape
    span, width = stat_left.shape[1:]
    any_spec = pl.BlockSpec(memory_space=pl.ANY)
    smem_spec = pl.BlockSpec(memory_space=pltpu.SMEM)
    dma = pltpu.SemaphoreType.DMA
    gather_sems = [dma((2, 4)), dma((2, 4)), dma((4,)), dma((4,))]
    update, first, second, left, right = pl.pallas_call(
        kernel,
        out_shape=(
            jax.ShapeDtypeStruct(grad.shape, bf16),
            jax.ShapeDtypeStruct(grad.shape, f32),
            jax.ShapeDtypeStruct(grad.shape, f32),
            jax.ShapeDtypeStruct((span, width), f32),
            jax.ShapeDtypeStruct((span, width), f32),
        ),
        in_specs=[smem_spec] * 2 + [any_spec] * 7,
        out_specs=[any_spec] * 5,
        scratch_shapes=[
            pltpu.VMEM((nblk, rows, cols), bf16),
            pltpu.VMEM((nblk, rows, cols), f32),
            pltpu.VMEM((nblk, rows, cols), f32),
            pltpu.VMEM((span, width), f32),
            pltpu.VMEM((span, width), f32),
            pltpu.VMEM((NY, span, width), bf16),
            pltpu.VMEM((width, cols), bf16),
            pltpu.VMEM((NS, rows, cols), bf16),
            pltpu.VMEM((NY, width, cols), bf16),
            pltpu.VMEM((width, cols), bf16),
            pltpu.VMEM((width, cols), bf16),
            pltpu.VMEM((NS, rows, cols), bf16),
            pltpu.VMEM((nblk, rows, cols), bf16),
            pltpu.VMEM((nblk, 128), f32),
            pltpu.VMEM((SMALL, 8, 128), f32),
            pltpu.VMEM((SMALL, 8, 128), f32),
            dma((7,)),
            dma((5,)),
            dma,
            dma((NX,)),
            dma,
            dma,
            *gather_sems,
            *gather_sems,
            dma((4,)),
            dma((4,)),
            dma((4,)),
            dma((4,)),
        ],
        compiler_params=pltpu.CompilerParams(
            collective_id=0, has_side_effects=True, vmem_limit_bytes=32 * 1024 * 1024
        ),
    )(
        owner_slot, inverse, grad, first_moment, second_moment, stat_left[0], stat_right[0],
        root_left[0], root_right[0],
    )
    return (update, first, second, left[None], right[None])


def solution(mesh):
    placed = (
        P(None, "shard", "rep"),
        P(None, "shard", "rep"),
        P(None, "shard", "rep"),
        P("shard", "rep", None),
        P("shard", "rep", None),
        P("shard", "rep", None),
        P("shard", None, "rep"),
        P(),
    )
    return jax.shard_map(
        per_device,
        mesh=mesh,
        in_specs=placed,
        out_specs=(
            P(None, "shard", "rep"),
            P(None, "shard", "rep"),
            P(None, "shard", "rep"),
            P("shard", "rep", None),
            P("shard", "rep", None),
        ),
        check_vma=False,
    )
```

time: 230 us -> 83.2 us (0.36)
  blocking collectives: 105 us -> 0 us
  waiting for transfers between devices: 82.3 us -> 0 us
  Pallas kernels: 0 us -> 69.2 us
  between operations: 14.1 us -> 0.67 us
  local copies, waits for them, and re-layouts: 1.2 us -> 12.9 us
  matrix products: 11.7 us -> 0 us
  starting transfers between devices: 11.7 us -> 0 us
  other arithmetic: 3.32 us -> 0.1 us
    psum x1 -> x0, blocking collectives: 75.1 us -> none  [per_device(): lax.psum((jnp.sum(adam * adam, axis=(1, 2)), jnp.sum(pieces * pieces, axi...]
    all_gather x2 -> x0, waiting for transfers between devices: 71.6 us -> none  [the longest x1 38.2 us: per_device(): lax.all_gather(left_part, 'rep', axis=1, tiled=True)]
    pallas_call x0 -> x1, Pallas kernels: none -> 69.2 us  [per_device(): pl.pallas_call(kernel, out_shape=(jax.ShapeDtypeStruct(grad.shape, bf16),...]
    all_to_all x1 -> x0, blocking collectives: 30.2 us -> none  [per_device(): lax.all_to_all(outgoing, 'shard', split_axis=1, concat_axis=2, tiled=True)]
    unnamed x15 -> x21, local copies, waits for them, and re-layouts: 0.9 us -> 12.9 us
    dot_general x6 -> x0, matrix products: 11.7 us -> none  [the longest x1 3.16 us: per_device(): jnp.einsum('cij,cjk->cik', lax.all_gather(left_part, 'rep', axis=1, tiled...]
    all_to_all x1 -> x0, starting transfers between devices: 11.7 us -> none  [per_device(): lax.all_to_all(outbound, 'shard', split_axis=1, concat_axis=1, tiled=True)]
    all_to_all x1 -> x0, waiting for transfers between devices: 10.6 us -> none  [per_device(): lax.all_to_all(outbound, 'shard', split_axis=1, concat_axis=1, tiled=True)]
  transfers between devices with their start and end apart: 3 -> 0, of which waited for: 3 -> 0; matrix products, arithmetic and copies ran while one was open for 3% -> 0% of each run, Pallas kernels for 0% -> 0%
where the time goes in v1:
time: 83.2 us; the launch traced here: 82.9 us
  Pallas kernels  69.2 us (83%)
  local copies, waits for them, and re-layouts  12.9 us (16%)
    pallas_call x1, Pallas kernels, per_device(): pl.pallas_call(kernel, out_shape=(jax.ShapeDtypeStruct(grad.shape, bf16),...  69.2 us
    unnamed x21, local copies, waits for them, and re-layouts  12.9 us

profile of v1, /device:TPU:1, one launch (start us, length us, event | category | flops | bytes accessed | tf_op | source)
XLA Modules:
  0.0 82.9 jit_solution(3400732780734647668)
XLA Ops:
  0.6 0.0 copy-start.7
  0.7 0.6 copy-done.7
  1.3 0.1 select_reduce_fusion
  1.4 0.0 copy-start
  1.4 1.2 %copy-done = f32[1,256,1024]{2,1,0:T(8,128)S(1)} copy-done((f32[1,256,1024]{2,1,0:T(8,128)S(1)}, f32[1,256,1024]{2,1,0:T(8,128)}, u32[]{:S(2)}) %copy-start) | copy-done | bytes 1048600
  2.6 0.0 copy-start.1
  2.6 1.2 %copy-done.1 = f32[1,256,1024]{2,1,0:T(8,128)S(1)} copy-done((f32[1,256,1024]{2,1,0:T(8,128)S(1)}, f32[1,256,1024]{2,1,0:T(8,128)}, u32[]{:S(2)}) %copy-start.1) | copy-done | bytes 1048600
  3.8 0.0 copy-start.2
  3.8 1.1 %copy-done.2 = f32[48,16,256]{2,1,0:T(8,128)S(1)} copy-done((f32[48,16,256]{2,1,0:T(8,128)S(1)}, f32[48,16,256]{2,1,0:T(8,128)}, u32[]{:S(2)}) %copy-start.2) | copy-done | bytes 786456
  5.0 0.0 copy-start.3
  5.0 1.1 %copy-done.3 = f32[48,16,256]{2,1,0:T(8,128)S(1)} copy-done((f32[48,16,256]{2,1,0:T(8,128)S(1)}, f32[48,16,256]{2,1,0:T(8,128)}, u32[]{:S(2)}) %copy-start.3) | copy-done | bytes 786456
  6.1 0.0 copy-start.4
  6.1 1.0 %copy-done.4 = bf16[1,256,1024]{2,1,0:T(8,128)(2,1)S(1)} copy-done((bf16[1,256,1024]{2,1,0:T(8,128)(2,1)S(1)}, bf16[1,256,1024]{2,1,0:T(8,128)(2,1)}, u32[]{:S(2)}) %copy-start.4) | copy-done | bytes 524312
  7.2 0.0 copy-start.5
  7.2 1.0 %copy-done.5 = bf16[1,1024,256]{2,1,0:T(8,128)(2,1)S(1)} copy-done((bf16[1,1024,256]{2,1,0:T(8,128)(2,1)S(1)}, bf16[1,1024,256]{2,1,0:T(8,128)(2,1)}, u32[]{:S(2)}) %copy-start.5) | copy-done | bytes 524312
  8.2 0.0 copy-start.6
  8.2 1.0 %copy-done.6 = bf16[48,16,256]{2,1,0:T(8,128)(2,1)S(1)} copy-done((bf16[48,16,256]{2,1,0:T(8,128)(2,1)S(1)}, bf16[48,16,256]{2,1,0:T(8,128)(2,1)}, u32[]{:S(2)}) %copy-start.6) | copy-done | bytes 393240
  9.2 69.2 %shard_map.119 = (bf16[48,16,256]{2,1,0:T(8,128)(2,1)S(1)}, f32[48,16,256]{2,1,0:T(8,128)S(1)}, f32[48,16,256]{2,1,0:T(8,128)S(1)}, f32[256,1024]{1,0:T(8,128)S(1)}, f32[256,1024]{1,0:T(8,128)S(1)}) custom-call(s32[48]{0:T(128)S(1)} %copy-done.7, s32[64]{0:T(128)S(1)} %broadcast_add_fusion.inv, bf16[48,16,256]{2,1,0:T(8,128)(2,1)S(1)} %copy-done.6, ...), custom_call_target="tpu_custom_call" | custom-call | tf_op jit(solution)/shard_map/pallas_call | solution.py:364
  78.4 0.7 copy.18
  79.2 0.9 %copy.19 = f32[48,16,256]{2,1,0:T(8,128)} copy(f32[48,16,256]{2,1,0:T(8,128)S(1)} %get-tuple-element.21) | data formatting | bytes 1572864
  80.0 0.9 %copy.20 = f32[48,16,256]{2,1,0:T(8,128)} copy(f32[48,16,256]{2,1,0:T(8,128)S(1)} %get-tuple-element.22) | data formatting | bytes 1572864
  80.9 1.0 %copy.21 = f32[1,256,1024]{2,1,0:T(8,128)} copy(f32[1,256,1024]{2,1,0:T(8,128)S(1)} %bitcast.7) | data formatting | bytes 2097152
  81.9 1.0 %copy.22 = f32[1,256,1024]{2,1,0:T(8,128)} copy(f32[1,256,1024]{2,1,0:T(8,128)S(1)} %bitcast.6) | data formatting | bytes 2097152
  (2 shorter events, 0.0 us)
Async XLA Ops:
  0.6 0.7 copy-start.7
  1.4 1.2 %copy-start = (f32[1,256,1024]{2,1,0:T(8,128)S(1)}, f32[1,256,1024]{2,1,0:T(8,128)}, u32[]{:S(2)}) copy-start(f32[1,256,1024]{2,1,0:T(8,128)} %param.11) | copy-start | bytes 3145732
  2.6 1.2 %copy-start.1 = (f32[1,256,1024]{2,1,0:T(8,128)S(1)}, f32[1,256,1024]{2,1,0:T(8,128)}, u32[]{:S(2)}) copy-start(f32[1,256,1024]{2,1,0:T(8,128)} %param.12) | copy-start | bytes 3145732
  3.8 1.1 %copy-start.2 = (f32[48,16,256]{2,1,0:T(8,128)S(1)}, f32[48,16,256]{2,1,0:T(8,128)}, u32[]{:S(2)}) copy-start(f32[48,16,256]{2,1,0:T(8,128)} %m1.1) | copy-start | bytes 2359300
  5.0 1.1 %copy-start.3 = (f32[48,16,256]{2,1,0:T(8,128)S(1)}, f32[48,16,256]{2,1,0:T(8,128)}, u32[]{:S(2)}) copy-start(f32[48,16,256]{2,1,0:T(8,128)} %m2.1) | copy-start | bytes 2359300
  6.1 1.0 %copy-start.4 = (bf16[1,256,1024]{2,1,0:T(8,128)(2,1)S(1)}, bf16[1,256,1024]{2,1,0:T(8,128)(2,1)}, u32[]{:S(2)}) copy-start(bf16[1,256,1024]{2,1,0:T(8,128)(2,1)} %param.13) | copy-start | bytes 1572868
  7.2 1.0 %copy-start.5 = (bf16[1,1024,256]{2,1,0:T(8,128)(2,1)S(1)}, bf16[1,1024,256]{2,1,0:T(8,128)(2,1)}, u32[]{:S(2)}) copy-start(bf16[1,1024,256]{2,1,0:T(8,128)(2,1)} %param.14) | copy-start | bytes 1572868
  8.2 1.0 %copy-start.6 = (bf16[48,16,256]{2,1,0:T(8,128)(2,1)S(1)}, bf16[48,16,256]{2,1,0:T(8,128)(2,1)}, u32[]{:S(2)}) copy-start(bf16[48,16,256]{2,1,0:T(8,128)(2,1)} %grad.1) | copy-start | bytes 1179652

commit v2 on v1

--- a/solution.py
+++ b/solution.py
@@ -20,6 +20,7 @@
 NS = NX * NZ * NC
 GROUP = NZ * NC
 X_ORDER = (0, 1, 3, 2)
+Z_ORDER = (1, 3, 2, 0)
 
 
 def remote(src, dst, send_sem, recv_sem, device):
@@ -121,12 +122,12 @@
 
 
 def kernel(
-    owner, inv, grad, m1, m2, stat_l, stat_r, root_l, root_r,
-    update_out, first_out, second_out, left_out, right_out,
-    gv, m1v, m2v, slv, srv, rlf, rrv, outb, gc, tv, pv, rc2, upv, acc, small_a, small_p,
+    inv, grad, m1, m2, stat_l, stat_r, root_l, root_r,
+    returned, factor_out, first_out, second_out, left_out, right_out,
+    gv, m1v, m2v, slv, srv, rlf, rrv, outb, gc, tv, pv, acc, small_a, small_p, norms, facv,
     in_sem, out_sem, bulk_send, bulk_recv, back_send, back_recv,
     g_os, g_or, g_fs, g_fr, l_os, l_or, l_fs, l_fr,
-    sa_send, sa_recv, sp_send, sp_recv,
+    sa_send, sa_recv, sp_send, sp_recv, norm_send, norm_recv,
 ):
     r = lax.axis_index("rep")
     s = lax.axis_index("shard")
@@ -187,16 +188,16 @@
         lax.fori_loop(1 if dx == 0 else 0, GROUP, body, 0)
 
     quarter = GROUP * 16
+    planes = [lax.rem(x + NX - dx, NX) for dx in X_ORDER]
     grads = ColumnGather(
-        gc,
-        [rows_of(lax.rem(x + NX - dx, NX), quarter) for dx in X_ORDER],
-        (g_os, g_or, g_fs, g_fr), r, s,
-    )
-    lefts = ColumnGather(rlf, [pl.ds(64 * k, 64) for k in range(4)], (l_os, l_or, l_fs, l_fr), r, s)
+        gc, [rows_of(plane, quarter) for plane in planes], (g_os, g_or, g_fs, g_fr), r, s
+    )
+    parts = [lax.rem(lax.div(zc, 4) + dz, 4) for dz in Z_ORDER]
+    lefts = ColumnGather(rlf, [rows_of(part, 64) for part in parts], (l_os, l_or, l_fs, l_fr), r, s)
 
     send_rows(X_ORDER[0])
-    for k in range(4):
-        lefts.send(k)
+    lefts.send(0)
+    lefts.send(1)
     for dx in X_ORDER[1:]:
         send_rows(dx)
 
@@ -229,73 +230,66 @@
     adam_sum.start("core", vec)
 
     def group_in(k):
-        plane = lax.rem(x + NX - X_ORDER[k], NX)
-        await_bytes(gc.at[r, rows_of(plane, quarter)], bulk_recv.at[plane])
+        await_bytes(gc.at[r, rows_of(planes[k], quarter)], bulk_recv.at[planes[k]])
 
     group_in(0)
     grads.send(0)
-    adam_sum.start("z", adam_sum.finish("core"))
     lefts.pass_on(0)
     lefts.pass_on(1)
+    adam_sum.start("z", adam_sum.finish("core"))
     group_in(1)
     grads.send(1)
+    grads.pass_on(0)
     adam_sum.start("x", adam_sum.finish("z"))
-    lefts.pass_on(2)
     group_in(2)
     grads.send(2)
-    lefts.pass_on(3)
+    grads.pass_on(1)
     group_in(3)
     grads.send(3)
     adam_sum.start("y", adam_sum.finish("x"))
-    for k in range(4):
-        grads.pass_on(k)
+    grads.pass_on(2)
+    grads.pass_on(3)
+    lefts.send(2)
+    lefts.send(3)
     adam_sq = adam_sum.finish("y")
-    for k in range(4):
-        lefts.last(k)
-    for k in range(4):
-        grads.last(k)
 
     loads[4].wait()
 
-    def right_rows(m, carry):
-        rows = rows_of(m, 256)
-        total = jnp.zeros((256, 256), f32)
+    def right_rows(k):
+        rows = rows_of(planes[k], quarter)
+        total = jnp.zeros((quarter, 256), f32)
         for q in range(NY):
             total += jnp.dot(gc[q, rows, :], rrv[pl.ds(256 * q, 256), :], preferred_element_type=f32)
         tv[rows, :] = total.astype(bf16)
-        return carry
-
-    lax.fori_loop(0, 4, right_rows, 0)
-
-    def left_rows(m, total):
-        part = jnp.dot(rlf[m], tv[...], preferred_element_type=f32).astype(bf16)
-        pv[rows_of(m, 256), :] = part
+
+    for k in range(NX):
+        grads.last(k)
+        right_rows(k)
+
+    def precondition(j):
+        rows = rows_of(parts[j], 64)
+        part = rlf[:, rows, :].reshape(256, 1024)
+        part = jnp.dot(part, tv[...], preferred_element_type=f32).astype(bf16)
+        pv[:, rows, :] = part.reshape(NX, 64, 256)
+
+        def body(i, carry):
+            plane = lax.rem(x + lax.div(i, 4), NX)
+            place = 4 * parts[j] + lax.rem(zc + i, 4)
+            remote(
+                pv.at[plane, rows_of(place, 16)], returned.at[s], back_send, back_recv,
+                (r, plane * GROUP + place),
+            ).start()
+            return carry
+
+        first = 0
+        if Z_ORDER[j] == 0:
+            pltpu.make_async_copy(pv.at[x, rows_of(zc, 16)], returned.at[s], back_recv).start()
+            first = 1
+        lax.fori_loop(first, 16, body, 0)
         wide = part.astype(f32)
-        return total + jnp.sum(wide * wide, axis=0, keepdims=True)
-
-    norm = lax.fori_loop(0, 4, left_rows, jnp.zeros((1, 256), f32))
-    norm = jnp.sum(norm, axis=1, keepdims=True)
-    block = inv[s]
-    lanes = lax.broadcasted_iota(jnp.int32, (8, 128), 1)
-    spot = jnp.where(lanes == block, jnp.broadcast_to(norm, (8, 128)), 0.0)
-    norm_sum = SmallSum(small_p, sp_send, sp_recv, r, s)
-    norm_sum.start("y", spot)
-
-    pltpu.make_async_copy(pv.at[rows_of(s, 16)], rc2.at[s], back_recv).start()
-    for dx in X_ORDER[::-1]:
-        plane = lax.rem(x + dx, NX)
-
-        def body(i, carry, plane=plane):
-            peer = plane * GROUP + lax.rem(zc + i, GROUP)
-            remote(pv.at[rows_of(peer, 16)], rc2.at[s], back_send, back_recv, (r, peer)).start()
-            return carry
-
-        lax.fori_loop(1 if dx == 0 else 0, GROUP, body, 0)
-
-    has = (block >= 0).astype(f32)
-    loads[5].wait()
-    loads[6].wait()
-    norm_sum.start("core", norm_sum.finish("y"))
+        return jnp.sum(wide * wide, axis=0, keepdims=True)
+
+    has = (inv[s] >= 0).astype(f32)
 
     def gram_left(j, carry):
         cols = rows_of(j, 256)
@@ -308,11 +302,6 @@
         slv[:, cols] = slv[:, cols] + has * total
         return carry
 
-    lax.fori_loop(0, 4, gram_left, 0)
-    store_left = pltpu.make_async_copy(slv, left_out, out_sem.at[2])
-    store_left.start()
-    norm_sum.start("z", norm_sum.finish("core"))
-
     def gram_right(q, carry):
         cols = rows_of(q, 256)
         total = lax.dot_general(
@@ -321,19 +310,38 @@
         srv[:, cols] = srv[:, cols] + has * total
         return carry
 
+    lefts.last(0)
+    norm = precondition(0)
+    lefts.last(1)
+    norm += precondition(1)
+    loads[5].wait()
+    lax.fori_loop(0, 4, gram_left, 0)
+    store_left = pltpu.make_async_copy(slv, left_out, out_sem.at[2])
+    store_left.start()
+    lefts.pass_on(2)
+    loads[6].wait()
     lax.fori_loop(0, 4, gram_right, 0)
     store_right = pltpu.make_async_copy(srv, right_out, out_sem.at[3])
     store_right.start()
-    norm_sum.start("x", norm_sum.finish("z"))
-    norm_sq = norm_sum.finish("x")
-
-    factor = -(jnp.sqrt(adam_sq) / (jnp.sqrt(norm_sq) + norm_eps))
-    await_bytes(rc2, back_recv)
-    for b in range(nblk):
-        scale = jnp.broadcast_to(factor[0:1, b : b + 1], (16, 256))
-        upv[b] = (scale * rc2[owner[b]].astype(f32)).astype(bf16)
-    store_update = pltpu.make_async_copy(upv, update_out, out_sem.at[4])
-    store_update.start()
+    lefts.pass_on(3)
+    lefts.last(2)
+    norm += precondition(2)
+    lefts.last(3)
+    norm += precondition(3)
+
+    norm = jnp.sum(norm, axis=1, keepdims=True)
+    lanes = lax.broadcasted_iota(jnp.int32, (8, 128), 1)
+    spot = jnp.where(lanes == inv[s], jnp.broadcast_to(norm, (8, 128)), 0.0)
+    norm_sum = SmallSum(small_p, sp_send, sp_recv, r, s)
+    norm_sum.start("y", spot)
+    norms[s] = norm_sum.finish("y")[:1]
+
+    def tell(i, carry):
+        ref = norms.at[s]
+        remote(ref, ref, norm_send, norm_recv, (r, lax.rem(s + i, NS))).start()
+        return carry
+
+    lax.fori_loop(1, NS, tell, 0)
 
     grads.drain()
     lefts.drain()
@@ -344,7 +352,51 @@
     store_second.wait()
     store_left.wait()
     store_right.wait()
-    store_update.wait()
+    others = norms.at[pl.ds(0, NS - 1)]
+    await_bytes(others, norm_send)
+    await_bytes(others, norm_recv)
+    norm_sq = jnp.sum(norms[...], axis=0)
+    facv[...] = -(jnp.sqrt(adam_sq) / (jnp.sqrt(norm_sq) + norm_eps))
+    store_factor = pltpu.make_async_copy(facv, factor_out, out_sem.at[4])
+    store_factor.start()
+    await_bytes(returned, back_recv)
+    store_factor.wait()
+
+
+def finish(
+    owner, returned, factor, first, second, left, right,
+    update_out, first_out, second_out, left_out, right_out,
+    rows, facv, upv, m1v, m2v, slv, srv, in_sem, out_sem,
+):
+    chain = (
+        (first, m1v, first_out), (second, m2v, second_out), (left, slv, left_out), (right, srv, right_out)
+    )
+    takes = [
+        pltpu.make_async_copy(src, via, in_sem.at[2 + i]) for i, (src, via, _) in enumerate(chain)
+    ]
+    gives = [
+        pltpu.make_async_copy(via, dst, out_sem.at[1 + i]) for i, (_, via, dst) in enumerate(chain)
+    ]
+    take = pltpu.make_async_copy(returned, rows, in_sem.at[0])
+    take_factor = pltpu.make_async_copy(factor, facv, in_sem.at[1])
+    take.start()
+    take_factor.start()
+    for copy in takes:
+        copy.start()
+    take_factor.wait()
+    take.wait()
+    scales = facv[...]
+    for b in range(upv.shape[0]):
+        scale = jnp.broadcast_to(scales[0:1, b : b + 1], upv.shape[1:])
+        upv[b] = (scale * rows[owner[b]].astype(f32)).astype(bf16)
+    give = pltpu.make_async_copy(upv, update_out, out_sem.at[0])
+    give.start()
+    for came, goes in zip(takes, gives):
+        came.wait()
+        goes.start()
+    for copy in gives:
+        copy.wait()
+    give.wait()
 
 
 def per_device(
@@ -361,17 +413,19 @@
     smem_spec = pl.BlockSpec(memory_space=pltpu.SMEM)
     dma = pltpu.SemaphoreType.DMA
     gather_sems = [dma((2, 4)), dma((2, 4)), dma((4,)), dma((4,))]
-    update, first, second, left, right = pl.pallas_call(
+    moments = [jax.ShapeDtypeStruct(grad.shape, f32)] * 2
+    stats = [jax.ShapeDtypeStruct((span, width), f32)] * 2
+    grant = 60 * 1024 * 1024
+    results = pl.pallas_call(
         kernel,
         out_shape=(
-            jax.ShapeDtypeStruct(grad.shape, bf16),
-            jax.ShapeDtypeStruct(grad.shape, f32),
-            jax.ShapeDtypeStruct(grad.shape, f32),
-            jax.ShapeDtypeStruct((span, width), f32),
-            jax.ShapeDtypeStruct((span, width), f32),
+            jax.ShapeDtypeStruct((NS, rows, cols), bf16),
+            jax.ShapeDtypeStruct((8, 128), f32),
+            *moments,
+            *stats,
         ),
-        in_specs=[smem_spec] * 2 + [any_spec] * 7,
-        out_specs=[any_spec] * 5,
+        in_specs=[smem_spec] + [any_spec] * 7,
+        out_specs=[any_spec] * 6,
         scratch_shapes=[
             pltpu.VMEM((nblk, rows, cols), bf16),
             pltpu.VMEM((nblk, rows, cols), f32),
@@ -383,12 +437,12 @@
             pltpu.VMEM((NS, rows, cols), bf16),
             pltpu.VMEM((NY, width, cols), bf16),
             pltpu.VMEM((width, cols), bf16),
-            pltpu.VMEM((width, cols), bf16),
-            pltpu.VMEM((NS, rows, cols), bf16),
-            pltpu.VMEM((nblk, rows, cols), bf16),
+            pltpu.VMEM((NX, width // NX, cols), bf16),
             pltpu.VMEM((nblk, 128), f32),
             pltpu.VMEM((SMALL, 8, 128), f32),
             pltpu.VMEM((SMALL, 8, 128), f32),
+            pltpu.VMEM((NS, 1, 128), f32),
+            pltpu.VMEM((8, 128), f32),
             dma((7,)),
             dma((5,)),
             dma,
@@ -401,14 +455,34 @@
             dma((4,)),
             dma((4,)),
             dma((4,)),
+            dma,
+            dma,
         ],
         compiler_params=pltpu.CompilerParams(
-            collective_id=0, has_side_effects=True, vmem_limit_bytes=32 * 1024 * 1024
+            collective_id=0, has_side_effects=True, vmem_limit_bytes=grant
         ),
     )(
-        owner_slot, inverse, grad, first_moment, second_moment, stat_left[0], stat_right[0],
+        inverse, grad, first_moment, second_moment, stat_left[0], stat_right[0],
         root_left[0], root_right[0],
     )
+    update, first, second, left, right = pl.pallas_call(
+        finish,
+        out_shape=(jax.ShapeDtypeStruct(grad.shape, bf16), *moments, *stats),
+        in_specs=[smem_spec] + [any_spec] * 6,
+        out_specs=[any_spec] * 5,
+        scratch_shapes=[
+            pltpu.VMEM((NS, rows, cols), bf16),
+            pltpu.VMEM((8, 128), f32),
+            pltpu.VMEM((nblk, rows, cols), bf16),
+            pltpu.VMEM((nblk, rows, cols), f32),
+            pltpu.VMEM((nblk, rows, cols), f32),
+            pltpu.VMEM((span, width), f32),
+            pltpu.VMEM((span, width), f32),
+            dma((6,)),
+            dma((5,)),
+        ],
+        compiler_params=pltpu.CompilerParams(vmem_limit_bytes=grant),
+    )(owner_slot, *results)
     return (update, first, second, left[None], right[None])
 
 

time: 83.2 us -> 72.1 us (0.87)
  local copies, waits for them, and re-layouts: 12.9 us -> 0.64 us
    unnamed x21 -> x2, local copies, waits for them, and re-layouts: 12.9 us -> 0.64 us
    pallas_call x1 -> x2, Pallas kernels: 69.2 us -> 70 us  [the longest x1 66.1 us: per_device(): pl.pallas_call(kernel, out_shape=(jax.ShapeDtypeStruct((NS, rows, cols),...]
where the time goes in v2:
time: 72.1 us; the launch traced here: 72 us
  Pallas kernels  70 us (97%)
    pallas_call x1, Pallas kernels, per_device(): pl.pallas_call(kernel, out_shape=(jax.ShapeDtypeStruct((NS, rows, cols),...  66.1 us
    pallas_call x1, Pallas kernels, per_device(): pl.pallas_call(finish, out_shape=(jax.ShapeDtypeStruct(grad.shape, bf16),...  3.99 us

profile of v2, /device:TPU:1, one launch (start us, length us, event | category | flops | bytes accessed | tf_op | source)
XLA Modules:
  0.0 72.0 jit_solution(17936133834131945286)
XLA Ops:
  0.6 0.0 copy-start
  0.7 0.6 copy-done
  1.3 0.1 select_reduce_fusion
  1.4 0.5 broadcast_add_fusion.inv
  1.9 66.1 %shard_map.119 = (bf16[64,16,256]{2,1,0:T(8,128)(2,1)}, f32[8,128]{1,0:T(8,128)}, f32[48,16,256]{2,1,0:T(8,128)}, f32[48,16,256]{2,1,0:T(8,128)}, f32[256,1024]{1,0:T(8,128)}, /*index=5*/f32[256,1024]{1,0:T(8,128)}) custom-call(s32[64]{0:T(128)} %broadcast_add_fusion.inv, bf16[48,16,256]{2,1,0:T(8,128)(2,1)} %grad.1, f32[48,16,256]{2,1,0:T(8,128)} %m1.1, ...), custom_call_target="tpu_custom_call" | custom-call | tf_op jit(solution)/shard_map/pallas_call | solution.py:419
  68.0 4.0 %shard_map.120 = (bf16[48,16,256]{2,1,0:T(8,128)(2,1)}, f32[48,16,256]{2,1,0:T(8,128)}, f32[48,16,256]{2,1,0:T(8,128)}, f32[256,1024]{1,0:T(8,128)}, f32[256,1024]{1,0:T(8,128)}) custom-call(s32[48]{0:T(128)} %owner.1, bf16[64,16,256]{2,1,0:T(8,128)(2,1)} %get-tuple-element.16.returned, f32[8,128]{1,0:T(8,128)} %get-tuple-element.17.factor, ...), custom_call_target="tpu_custom_call" | custom-call | tf_op jit(solution)/shard_map/pallas_call | solution.py:468
  (1 shorter events, 0.0 us)
Async XLA Ops:
  0.6 0.7 copy-start

commit v3 on v2

--- a/solution.py
+++ b/solution.py
@@ -19,8 +19,9 @@
 NX, NZ, NC, NY = 4, 8, 2, 4
 NS = NX * NZ * NC
 GROUP = NZ * NC
-X_ORDER = (0, 1, 3, 2)
-Z_ORDER = (1, 3, 2, 0)
+Z_NEAR = (0, 1, 7, 2, 6, 3, 5, 4)
+Z_FAR = (2, 1, 3, 0)
+EARLY, FILL, LAG = 3, 2, 2
 
 
 def remote(src, dst, send_sem, recv_sem, device):
@@ -51,18 +52,20 @@
         self.down = lax.rem(r + NY - 1, NY)
         self.opposite = lax.rem(r + 2, NY)
 
+    def chunk(self, q, k):
+        return self.buf.at[q, :, self.rows[k]]
+
     def own(self, k, way):
-        ref = self.buf.at[self.r, self.rows[k]]
+        ref = self.chunk(self.r, k)
         target = (self.up, self.down)[way]
         return remote(ref, ref, self.own_send.at[way, k], self.own_recv.at[way, k], (target, self.s))
 
     def arrived(self, k, way):
-        ref = self.buf.at[(self.down, self.up)[way], self.rows[k]]
-        await_bytes(ref, self.own_recv.at[way, k])
+        await_bytes(self.chunk((self.down, self.up)[way], k), self.own_recv.at[way, k])
 
     def forward(self, k):
         way = k % 2
-        ref = self.buf.at[(self.down, self.up)[way], self.rows[k]]
+        ref = self.chunk((self.down, self.up)[way], k)
         target = (self.up, self.down)[way]
         return remote(ref, ref, self.fwd_send.at[k], self.fwd_recv.at[k], (target, self.s))
 
@@ -71,16 +74,15 @@
         self.own(k, 1).start()
 
     def pass_on(self, k):
-        self.arrived(k, 0)
-        self.arrived(k, 1)
+        self.arrived(k, k % 2)
         self.forward(k).start()
 
     def last(self, k):
-        ref = self.buf.at[self.opposite, self.rows[k]]
-        await_bytes(ref, self.fwd_recv.at[k])
+        self.arrived(k, 1 - k % 2)
+        await_bytes(self.chunk(self.opposite, k), self.fwd_recv.at[k])
 
     def drain(self):
-        for k in range(4):
+        for k in range(len(self.rows)):
             self.own(k, 0).wait_send()
             self.own(k, 1).wait_send()
             self.forward(k).wait_send()
@@ -124,26 +126,31 @@
 def kernel(
     inv, grad, m1, m2, stat_l, stat_r, root_l, root_r,
     returned, factor_out, first_out, second_out, left_out, right_out,
-    gv, m1v, m2v, slv, srv, rlf, rrv, outb, gc, tv, pv, acc, small_a, small_p, norms, facv,
+    gv, m1v, m2v, slv, srv, rlv, rrv, outb, gc, tv, pv, ship, acc, small_a, small_p, norms, facv,
     in_sem, out_sem, bulk_send, bulk_recv, back_send, back_recv,
-    g_os, g_or, g_fs, g_fr, l_os, l_or, l_fs, l_fr,
+    g_os, g_or, g_fs, g_fr, l_send, l_recv, r_send, r_recv, ship_send, ship_recv,
     sa_send, sa_recv, sp_send, sp_recv, norm_send, norm_recv,
 ):
     r = lax.axis_index("rep")
     s = lax.axis_index("shard")
     x = lax.div(s, GROUP)
     zc = lax.rem(s, GROUP)
+    z, c = lax.div(zc, NC), lax.rem(zc, NC)
     nblk = gv.shape[0]
+    side = lax.rem(r, 2)
+    left_mate = r + 1 - 2 * side
+    right_mate = NY - 1 - r
+    base = r - side
 
     def load(i, src, dst):
         return pltpu.make_async_copy(src, dst, in_sem.at[i])
 
     loads = (
         load(0, grad, gv),
-        load(1, root_l, rlf.at[r]),
-        load(2, m1, m1v),
-        load(3, m2, m2v),
-        load(4, root_r, rrv),
+        load(1, root_l, rlv.at[side]),
+        load(2, root_r, rrv.at[0]),
+        load(3, m1, m1v),
+        load(4, m2, m2v),
         load(5, stat_l, slv),
         load(6, stat_r, srv),
     )
@@ -172,37 +179,50 @@
 
     lax.fori_loop(0, NS, pick, 0, unroll=4)
     loads[1].wait()
+    loads[2].wait()
     pl.semaphore_wait(barrier, NS - 1 + NY - 1)
 
-    mine = gc.at[r, rows_of(s, 16)]
-    pltpu.make_async_copy(outb.at[s], mine, bulk_recv.at[x]).start()
-
-    def send_rows(dx):
-        plane = lax.rem(x + dx, NX)
+    mine = gc.at[r, x, rows_of(zc, 16)]
+    pltpu.make_async_copy(outb.at[s], mine, bulk_recv.at[z]).start()
+
+    def send_rows(dz):
+        there = lax.rem(z + dz, NZ) * NC
 
         def body(i, carry):
-            peer = plane * GROUP + lax.rem(zc + i, GROUP)
-            remote(outb.at[peer], mine, bulk_send, bulk_recv.at[x], (r, peer)).start()
+            peer = lax.rem(x + lax.div(i, NC), NX) * GROUP + there + lax.rem(c + i, NC)
+            remote(outb.at[peer], mine, bulk_send, bulk_recv.at[z], (r, peer)).start()
             return carry
 
-        lax.fori_loop(1 if dx == 0 else 0, GROUP, body, 0)
-
-    quarter = GROUP * 16
-    planes = [lax.rem(x + NX - dx, NX) for dx in X_ORDER]
-    grads = ColumnGather(
-        gc, [rows_of(plane, quarter) for plane in planes], (g_os, g_or, g_fs, g_fr), r, s
-    )
-    parts = [lax.rem(lax.div(zc, 4) + dz, 4) for dz in Z_ORDER]
-    lefts = ColumnGather(rlf, [rows_of(part, 64) for part in parts], (l_os, l_or, l_fs, l_fr), r, s)
-
-    send_rows(X_ORDER[0])
-    lefts.send(0)
-    lefts.send(1)
-    for dx in X_ORDER[1:]:
-        send_rows(dx)
-
-    loads[2].wait()
+        lax.fori_loop(1 if dz == 0 else 0, NX * NC, body, 0)
+
+    quarters = [rows_of(lax.rem(lax.div(z, 2) + dq, 4), 64) for dq in Z_FAR]
+
+    def left_root(j, i):
+        ref = rlv.at[i, quarters[j]]
+        return remote(ref, ref, l_send.at[j], l_recv.at[j], (left_mate, s))
+
+    def right_root(j):
+        rows = pl.ds(256 * j, 256)
+        return remote(
+            rrv.at[0, rows], rrv.at[1, rows], r_send.at[j], r_recv.at[j], (right_mate, s)
+        )
+
+    def swap_roots(j):
+        left_root(j, side).start()
+        right_root(j).start()
+
+    near = [lax.rem(z + NZ - dz, NZ) for dz in Z_NEAR]
+    grads = ColumnGather(gc, [rows_of(other, 32) for other in near], (g_os, g_or, g_fs, g_fr), r, s)
+
+    for dz in Z_NEAR[:EARLY]:
+        send_rows(dz)
+    for j in range(FILL):
+        swap_roots(j)
+    for dz in Z_NEAR[EARLY:]:
+        send_rows(dz)
+
     loads[3].wait()
+    loads[4].wait()
 
     def adam(b, carry):
         g = gv[b].astype(f32)
@@ -229,65 +249,61 @@
     adam_sum = SmallSum(small_a, sa_send, sa_recv, r, s)
     adam_sum.start("core", vec)
 
-    def group_in(k):
-        await_bytes(gc.at[r, rows_of(planes[k], quarter)], bulk_recv.at[planes[k]])
-
-    group_in(0)
-    grads.send(0)
-    lefts.pass_on(0)
-    lefts.pass_on(1)
-    adam_sum.start("z", adam_sum.finish("core"))
-    group_in(1)
-    grads.send(1)
-    grads.pass_on(0)
-    adam_sum.start("x", adam_sum.finish("z"))
-    group_in(2)
-    grads.send(2)
-    grads.pass_on(1)
-    group_in(3)
-    grads.send(3)
-    adam_sum.start("y", adam_sum.finish("x"))
-    grads.pass_on(2)
-    grads.pass_on(3)
-    lefts.send(2)
-    lefts.send(3)
-    adam_sq = adam_sum.finish("y")
-
-    loads[4].wait()
+    for k in range(NZ):
+        await_bytes(grads.chunk(r, k), bulk_recv.at[near[k]])
+        grads.send(k)
+        if k >= LAG:
+            grads.pass_on(k - LAG)
+        if k == 1:
+            adam_sum.start("z", adam_sum.finish("core"))
+        if k == 4:
+            adam_sum.start("x", adam_sum.finish("z"))
+        if k == 6:
+            adam_sum.start("y", adam_sum.finish("x"))
+    for k in range(NZ - LAG, NZ):
+        grads.pass_on(k)
+    for j in range(FILL, 4):
+        swap_roots(j)
 
     def right_rows(k):
-        rows = rows_of(planes[k], quarter)
-        total = jnp.zeros((quarter, 256), f32)
+        total = jnp.zeros((NX * 32, 256), f32)
         for q in range(NY):
-            total += jnp.dot(gc[q, rows, :], rrv[pl.ds(256 * q, 256), :], preferred_element_type=f32)
-        tv[rows, :] = total.astype(bf16)
-
-    for k in range(NX):
+            part = gc[q, :, grads.rows[k], :].reshape(NX * 32, 256)
+            total += jnp.dot(part, rrv[0, pl.ds(256 * q, 256), :], preferred_element_type=f32)
+        tv[:, grads.rows[k], :] = total.astype(bf16).reshape(NX, 32, 256)
+
+    for k in range(NZ):
         grads.last(k)
         right_rows(k)
 
-    def precondition(j):
-        rows = rows_of(parts[j], 64)
-        part = rlf[:, rows, :].reshape(256, 1024)
-        part = jnp.dot(part, tv[...], preferred_element_type=f32).astype(bf16)
-        pv[:, rows, :] = part.reshape(NX, 64, 256)
-
+    def give_back(plane, j):
         def body(i, carry):
-            plane = lax.rem(x + lax.div(i, 4), NX)
-            place = 4 * parts[j] + lax.rem(zc + i, 4)
-            remote(
-                pv.at[plane, rows_of(place, 16)], returned.at[s], back_send, back_recv,
-                (r, plane * GROUP + place),
-            ).start()
+            place = 4 * lax.rem(lax.div(z, 2) + Z_FAR[j], 4) + lax.rem(zc + i, 4)
+            peer = plane * GROUP + place
+            src = pv.at[plane, rows_of(place, 16)]
+            dst = returned.at[s]
+
+            @pl.when(peer != s)
+            def _():
+                remote(src, dst, back_send, back_recv, (r, peer)).start()
+
+            @pl.when(peer == s)
+            def _():
+                pltpu.make_async_copy(src, dst, back_recv).start()
+
             return carry
 
-        first = 0
-        if Z_ORDER[j] == 0:
-            pltpu.make_async_copy(pv.at[x, rows_of(zc, 16)], returned.at[s], back_recv).start()
-            first = 1
-        lax.fori_loop(first, 16, body, 0)
+        lax.fori_loop(0, 4, body, 0)
+
+    def squares(part):
         wide = part.astype(f32)
         return jnp.sum(wide * wide, axis=0, keepdims=True)
+
+    part = jnp.dot(rlv[side], tv[...].reshape(1024, 256), preferred_element_type=f32).astype(bf16)
+    pv[r] = part
+    for j in range(4):
+        give_back(r, j)
+    norm = squares(part)
 
     has = (inv[s] >= 0).astype(f32)
 
@@ -296,8 +312,7 @@
         total = jnp.zeros((256, 256), f32)
         for q in range(NY):
             total += lax.dot_general(
-                gc[q, rows_of(r, 256), :], gc[q, cols, :], (((1,), (1,)), ((), ())),
-                preferred_element_type=f32,
+                gc[q, r], gc[q, j], (((1,), (1,)), ((), ())), preferred_element_type=f32
             )
         slv[:, cols] = slv[:, cols] + has * total
         return carry
@@ -305,29 +320,58 @@
     def gram_right(q, carry):
         cols = rows_of(q, 256)
         total = lax.dot_general(
-            gc[r], gc[q], (((0,), (0,)), ((), ())), preferred_element_type=f32
+            gc[r].reshape(1024, 256), gc[q].reshape(1024, 256), (((0,), (0,)), ((), ())),
+            preferred_element_type=f32,
         )
         srv[:, cols] = srv[:, cols] + has * total
         return carry
 
-    lefts.last(0)
-    norm = precondition(0)
-    lefts.last(1)
-    norm += precondition(1)
+    def mate_rows(j, norm):
+        left_root(j, 1 - side).wait_recv()
+        part = jnp.dot(
+            rlv[1 - side, quarters[j], :], tv[...].reshape(1024, 256), preferred_element_type=f32
+        ).astype(bf16)
+        pv[left_mate, quarters[j], :] = part
+        give_back(left_mate, j)
+        return norm + squares(part)
+
+    norm = mate_rows(0, norm)
     loads[5].wait()
     lax.fori_loop(0, 4, gram_left, 0)
     store_left = pltpu.make_async_copy(slv, left_out, out_sem.at[2])
     store_left.start()
-    lefts.pass_on(2)
+    norm = mate_rows(1, norm)
     loads[6].wait()
     lax.fori_loop(0, 4, gram_right, 0)
     store_right = pltpu.make_async_copy(srv, right_out, out_sem.at[3])
     store_right.start()
-    lefts.pass_on(3)
-    lefts.last(2)
-    norm += precondition(2)
-    lefts.last(3)
-    norm += precondition(3)
+    norm = mate_rows(2, norm)
+    norm = mate_rows(3, norm)
+
+    for j in range(4):
+        right_root(j).wait_recv()
+
+    def right_mate_rows(m, carry):
+        total = jnp.zeros((256, 256), f32)
+        for q in range(NY):
+            total += jnp.dot(gc[q, m], rrv[1, pl.ds(256 * q, 256), :], preferred_element_type=f32)
+        tv[m] = total.astype(bf16)
+        return carry
+
+    lax.fori_loop(0, NX, right_mate_rows, 0)
+
+    def shipment(j):
+        return remote(
+            ship.at[:, quarters[j]], pv.at[pl.ds(base, 2), quarters[j]],
+            ship_send.at[j], ship_recv.at[j], (right_mate, s),
+        )
+
+    for i in range(2):
+        part = jnp.dot(rlv[i], tv[...].reshape(1024, 256), preferred_element_type=f32).astype(bf16)
+        ship[i] = part
+        norm += squares(part)
+    for j in range(4):
+        shipment(j).start()
 
     norm = jnp.sum(norm, axis=1, keepdims=True)
     lanes = lax.broadcasted_iota(jnp.int32, (8, 128), 1)
@@ -342,16 +386,25 @@
         return carry
 
     lax.fori_loop(1, NS, tell, 0)
+    for j in range(4):
+        arriving = pv.at[pl.ds(2 - base, 2), quarters[j]]
+        await_bytes(arriving, ship_recv.at[j])
+        give_back(2 - base, j)
+        give_back(3 - base, j)
 
     grads.drain()
-    lefts.drain()
-    sent = gc.at[0, pl.ds(0, (NS - 1) * 16)]
+    for j in range(4):
+        left_root(j, side).wait_send()
+        right_root(j).wait_send()
+        shipment(j).wait_send()
+    sent = outb.at[pl.ds(0, NS - 1)]
     await_bytes(sent, bulk_send)
     await_bytes(sent, back_send)
     store_first.wait()
     store_second.wait()
     store_left.wait()
     store_right.wait()
+    adam_sq = adam_sum.finish("y")
     others = norms.at[pl.ds(0, NS - 1)]
     await_bytes(others, norm_send)
     await_bytes(others, norm_recv)
@@ -412,7 +465,6 @@
     any_spec = pl.BlockSpec(memory_space=pl.ANY)
     smem_spec = pl.BlockSpec(memory_space=pltpu.SMEM)
     dma = pltpu.SemaphoreType.DMA
-    gather_sems = [dma((2, 4)), dma((2, 4)), dma((4,)), dma((4,))]
     moments = [jax.ShapeDtypeStruct(grad.shape, f32)] * 2
     stats = [jax.ShapeDtypeStruct((span, width), f32)] * 2
     grant = 60 * 1024 * 1024
@@ -432,12 +484,13 @@
             pltpu.VMEM((nblk, rows, cols), f32),
             pltpu.VMEM((span, width), f32),
             pltpu.VMEM((span, width), f32),
-            pltpu.VMEM((NY, span, width), bf16),
-            pltpu.VMEM((width, cols), bf16),
+            pltpu.VMEM((2, span, width), bf16),
+            pltpu.VMEM((2, width, cols), bf16),
             pltpu.VMEM((NS, rows, cols), bf16),
-            pltpu.VMEM((NY, width, cols), bf16),
-            pltpu.VMEM((width, cols), bf16),
+            pltpu.VMEM((NY, NX, width // NX, cols), bf16),
             pltpu.VMEM((NX, width // NX, cols), bf16),
+            pltpu.VMEM((NX, width // NX, cols), bf16),
+            pltpu.VMEM((2, width // NX, cols), bf16),
             pltpu.VMEM((nblk, 128), f32),
             pltpu.VMEM((SMALL, 8, 128), f32),
             pltpu.VMEM((SMALL, 8, 128), f32),
@@ -446,11 +499,14 @@
             dma((7,)),
             dma((5,)),
             dma,
-            dma((NX,)),
+            dma((NZ,)),
             dma,
             dma,
-            *gather_sems,
-            *gather_sems,
+            dma((2, NZ)),
+            dma((2, NZ)),
+            dma((NZ,)),
+            dma((NZ,)),
+            *[dma((4,))] * 6,
             dma((4,)),
             dma((4,)),
             dma((4,)),

time: 72.1 us -> 66.6 us (0.924)
  Pallas kernels: 70 us -> 64 us
    pallas_call x1, Pallas kernels: 66.1 us -> 60 us  [per_device(): pl.pallas_call(kernel, out_shape=(jax.ShapeDtypeStruct((NS, rows, cols),...]
where the time goes in v3:
time: 66.6 us; the launch traced here: 65.9 us
  Pallas kernels  64 us (96%)
    pallas_call x1, Pallas kernels, per_device(): pl.pallas_call(kernel, out_shape=(jax.ShapeDtypeStruct((NS, rows, cols),...  60 us
    pallas_call x1, Pallas kernels, per_device(): pl.pallas_call(finish, out_shape=(jax.ShapeDtypeStruct(grad.shape, bf16),...  3.99 us

profile of v3, /device:TPU:1, one launch (start us, length us, event | category | flops | bytes accessed | tf_op | source)
XLA Modules:
  0.0 65.9 jit_solution(489264143812742975)
XLA Ops:
  0.6 0.0 copy-start
  0.7 0.6 copy-done
  1.3 0.1 select_reduce_fusion
  1.4 0.5 broadcast_add_fusion.inv
  1.9 60.0 %shard_map.119 = (bf16[64,16,256]{2,1,0:T(8,128)(2,1)}, f32[8,128]{1,0:T(8,128)}, f32[48,16,256]{2,1,0:T(8,128)}, f32[48,16,256]{2,1,0:T(8,128)}, f32[256,1024]{1,0:T(8,128)}, /*index=5*/f32[256,1024]{1,0:T(8,128)}) custom-call(s32[64]{0:T(128)} %broadcast_add_fusion.inv, bf16[48,16,256]{2,1,0:T(8,128)(2,1)} %grad.1, f32[48,16,256]{2,1,0:T(8,128)} %m1.1, ...), custom_call_target="tpu_custom_call" | custom-call | tf_op jit(solution)/shard_map/pallas_call | solution.py:471
  61.9 4.0 %shard_map.120 = (bf16[48,16,256]{2,1,0:T(8,128)(2,1)}, f32[48,16,256]{2,1,0:T(8,128)}, f32[48,16,256]{2,1,0:T(8,128)}, f32[256,1024]{1,0:T(8,128)}, f32[256,1024]{1,0:T(8,128)}) custom-call(s32[48]{0:T(128)} %owner.1, bf16[64,16,256]{2,1,0:T(8,128)(2,1)} %get-tuple-element.16.returned, f32[8,128]{1,0:T(8,128)} %get-tuple-element.17.factor, ...), custom_call_target="tpu_custom_call" | custom-call | tf_op jit(solution)/shard_map/pallas_call | solution.py:524
  (1 shorter events, 0.0 us)
Async XLA Ops:
  0.6 0.7 copy-start

commit v4 on v3

--- a/solution.py
+++ b/solution.py
@@ -21,7 +21,7 @@
 GROUP = NZ * NC
 Z_NEAR = (0, 1, 7, 2, 6, 3, 5, 4)
 Z_FAR = (2, 1, 3, 0)
-EARLY, FILL, LAG = 3, 2, 2
+EARLY, FILL_LEFT, FILL_RIGHT, LAG = 3, 3, 4, 2
 
 
 def remote(src, dst, send_sem, recv_sem, device):
@@ -124,10 +124,10 @@
 
 
 def kernel(
-    inv, grad, m1, m2, stat_l, stat_r, root_l, root_r,
+    owner, grad, m1, m2, stat_l, stat_r, root_l, root_r,
     returned, factor_out, first_out, second_out, left_out, right_out,
-    gv, m1v, m2v, slv, srv, rlv, rrv, outb, gc, tv, pv, ship, acc, small_a, small_p, norms, facv,
-    in_sem, out_sem, bulk_send, bulk_recv, back_send, back_recv,
+    gv, m1v, m2v, slv, srv, rlv, rrv, outb, gc, tv, tv2, pv, ship, acc, small_a, small_p, norms, facv,
+    invv, inv, inv_sem, word, in_sem, out_sem, bulk_send, bulk_recv, back_send, back_recv,
     g_os, g_or, g_fs, g_fr, l_send, l_recv, r_send, r_recv, ship_send, ship_recv,
     sa_send, sa_recv, sp_send, sp_recv, norm_send, norm_recv,
 ):
@@ -159,28 +159,33 @@
 
     barrier = pltpu.get_barrier_semaphore()
 
-    def greet(i, carry):
-        pl.semaphore_signal(
-            barrier, inc=1, device_id=(r, lax.rem(s + i, NS)), device_id_type=MESH
-        )
-        return carry
-
-    lax.fori_loop(1, NS, greet, 0)
-    for step in range(1, NY):
-        pl.semaphore_signal(
-            barrier, inc=1, device_id=(lax.rem(r + step, NY), s), device_id_type=MESH
-        )
-
+    def at(dx, dz, other=0):
+        there = lax.rem(x + dx + NX, NX) * GROUP + lax.rem(z + dz + NZ, NZ) * NC
+        return (r, there + lax.rem(c + other, NC))
+
+    hellos = [(lax.rem(r + step, NY), s) for step in range(1, NY)]
+    hellos += [at(0, 0, 1), at(1, 0), at(-1, 0), at(0, 1), at(0, -1)]
+    for device in hellos:
+        pl.semaphore_signal(barrier, inc=1, device_id=device, device_id_type=MESH)
+
+    lanes = lax.broadcasted_iota(jnp.int32, (8, 128), 1)
+    blocks = jnp.full((8, 128), -1, jnp.int32)
+    for b in range(nblk):
+        blocks = jnp.where(lanes == owner[b], b, blocks)
+    invv[...] = blocks
+    invert = pltpu.make_async_copy(invv, inv, inv_sem)
+    invert.start()
     loads[0].wait()
+    invert.wait()
 
     def pick(slot, carry):
-        outb[slot] = gv[jnp.maximum(inv[slot], 0)]
+        outb[slot] = gv[jnp.maximum(inv[0, slot], 0)]
         return carry
 
     lax.fori_loop(0, NS, pick, 0, unroll=4)
     loads[1].wait()
     loads[2].wait()
-    pl.semaphore_wait(barrier, NS - 1 + NY - 1)
+    pl.semaphore_wait(barrier, len(hellos))
 
     mine = gc.at[r, x, rows_of(zc, 16)]
     pltpu.make_async_copy(outb.at[s], mine, bulk_recv.at[z]).start()
@@ -207,19 +212,39 @@
             rrv.at[0, rows], rrv.at[1, rows], r_send.at[j], r_recv.at[j], (right_mate, s)
         )
 
-    def swap_roots(j):
-        left_root(j, side).start()
-        right_root(j).start()
-
     near = [lax.rem(z + NZ - dz, NZ) for dz in Z_NEAR]
     grads = ColumnGather(gc, [rows_of(other, 32) for other in near], (g_os, g_or, g_fs, g_fr), r, s)
 
-    for dz in Z_NEAR[:EARLY]:
-        send_rows(dz)
-    for j in range(FILL):
-        swap_roots(j)
-    for dz in Z_NEAR[EARLY:]:
-        send_rows(dz)
+    for j in range(FILL_RIGHT):
+        right_root(j).start()
+        if j < FILL_LEFT:
+            left_root(j, side).start()
+
+    def say(i, device):
+        pl.semaphore_signal(word.at[i], inc=1, device_id=device, device_id_type=MESH)
+
+    def hear(i):
+        pl.semaphore_wait(word.at[i], 1)
+
+    say(0, at(1, 0))
+    say(1, at(-1, 0))
+    hear(0)
+    hear(1)
+    say(2, at(1, 0))
+    hear(2)
+    say(3, at(0, 1))
+    say(4, at(0, -1))
+    send_rows(0)
+    for step in range(1, 4):
+        hear(2 * step + 1)
+        hear(2 * step + 2)
+        say(2 * step + 3, at(0, 1))
+        if step < 3:
+            say(2 * step + 4, at(0, -1))
+        send_rows(step)
+        send_rows(NZ - step)
+    hear(9)
+    send_rows(4)
 
     loads[3].wait()
     loads[4].wait()
@@ -262,16 +287,23 @@
             adam_sum.start("y", adam_sum.finish("x"))
     for k in range(NZ - LAG, NZ):
         grads.pass_on(k)
-    for j in range(FILL, 4):
-        swap_roots(j)
+    for j in range(FILL_RIGHT, 4):
+        right_root(j).start()
+    for j in range(FILL_LEFT, 4):
+        left_root(j, side).start()
 
     def right_rows(k):
-        total = jnp.zeros((NX * 32, 256), f32)
-        for q in range(NY):
-            part = gc[q, :, grads.rows[k], :].reshape(NX * 32, 256)
-            total += jnp.dot(part, rrv[0, pl.ds(256 * q, 256), :], preferred_element_type=f32)
-        tv[:, grads.rows[k], :] = total.astype(bf16).reshape(NX, 32, 256)
-
+        parts = [gc[q, :, grads.rows[k], :].reshape(NX * 32, 256) for q in range(NY)]
+        for i, out in enumerate((tv, tv2)):
+            total = jnp.zeros((NX * 32, 256), f32)
+            for q in range(NY):
+                total += jnp.dot(
+                    parts[q], rrv[i, pl.ds(256 * q, 256), :], preferred_element_type=f32
+                )
+            out[:, grads.rows[k], :] = total.astype(bf16).reshape(NX, 32, 256)
+
+    for j in range(4):
+        right_root(j).wait_recv()
     for k in range(NZ):
         grads.last(k)
         right_rows(k)
@@ -299,13 +331,7 @@
         wide = part.astype(f32)
         return jnp.sum(wide * wide, axis=0, keepdims=True)
 
-    part = jnp.dot(rlv[side], tv[...].reshape(1024, 256), preferred_element_type=f32).astype(bf16)
-    pv[r] = part
-    for j in range(4):
-        give_back(r, j)
-    norm = squares(part)
-
-    has = (inv[s] >= 0).astype(f32)
+    has = (inv[0, s] >= 0).astype(f32)
 
     def gram_left(j, carry):
         cols = rows_of(j, 256)
@@ -326,77 +352,89 @@
         srv[:, cols] = srv[:, cols] + has * total
         return carry
 
-    def mate_rows(j, norm):
-        left_root(j, 1 - side).wait_recv()
-        part = jnp.dot(
-            rlv[1 - side, quarters[j], :], tv[...].reshape(1024, 256), preferred_element_type=f32
+    def product(left, right):
+        return jnp.dot(
+            left, right[...].reshape(1024, 256), preferred_element_type=f32
         ).astype(bf16)
-        pv[left_mate, quarters[j], :] = part
-        give_back(left_mate, j)
-        return norm + squares(part)
-
-    norm = mate_rows(0, norm)
+
+    def shipment(i, j):
+        plane = (r, left_mate)[i]
+        return remote(
+            ship.at[i, quarters[j]], pv.at[plane, quarters[j]], ship_send.at[i, j],
+            ship_recv.at[i, j], (right_mate, s),
+        )
+
+    def shipped(i, j):
+        plane = (right_mate, 3 - left_mate)[i]
+        await_bytes(pv.at[plane, quarters[j]], ship_recv.at[i, j])
+        give_back(plane, j)
+
+    part = product(rlv[side], tv2)
+    ship[0] = part
+    for j in range(4):
+        shipment(0, j).start()
+    norm = squares(part)
+    part = product(rlv[side], tv)
+    pv[r] = part
+    for j in range(4):
+        give_back(r, j)
+    norm += squares(part)
+
+    def mate_rows(pair):
+        for j in pair:
+            left_root(j, 1 - side).wait_recv()
+        left = jnp.concatenate([rlv[1 - side, quarters[j], :] for j in pair], axis=0)
+        away = product(left, tv2)
+        for n, j in enumerate(pair):
+            ship[1, quarters[j], :] = away[64 * n : 64 * n + 64]
+            shipment(1, j).start()
+        here = product(left, tv)
+        for n, j in enumerate(pair):
+            pv[left_mate, quarters[j], :] = here[64 * n : 64 * n + 64]
+            give_back(left_mate, j)
+        return squares(away) + squares(here)
+
+    norm += mate_rows((0, 1))
+    norm += mate_rows((2, 3))
+
+    norm = jnp.sum(norm, axis=1, keepdims=True)
+    spot = jnp.where(lanes == inv[0, s], jnp.broadcast_to(norm, (8, 128)), 0.0)
+    norm_sum = SmallSum(small_p, sp_send, sp_recv, r, s)
+    norm_sum.start("y", spot)
+    norms[s] = norm_sum.finish("y")[:1]
+
+    def tell(i, carry):
+        far = lax.rem(z + NZ // 2 + lax.div(i, NX * NC), NZ) * NC
+        peer = lax.rem(x + 2 + lax.div(lax.rem(i, NX * NC), NC), NX) * GROUP + far + lax.rem(c + i, NC)
+        ref = norms.at[s]
+
+        @pl.when(peer != s)
+        def _():
+            remote(ref, ref, norm_send, norm_recv, (r, peer)).start()
+
+        return carry
+
+    lax.fori_loop(0, NS, tell, 0, unroll=4)
+    for j in range(4):
+        shipped(0, j)
+    for j in range(4):
+        shipped(1, j)
+
     loads[5].wait()
     lax.fori_loop(0, 4, gram_left, 0)
     store_left = pltpu.make_async_copy(slv, left_out, out_sem.at[2])
     store_left.start()
-    norm = mate_rows(1, norm)
     loads[6].wait()
     lax.fori_loop(0, 4, gram_right, 0)
     store_right = pltpu.make_async_copy(srv, right_out, out_sem.at[3])
     store_right.start()
-    norm = mate_rows(2, norm)
-    norm = mate_rows(3, norm)
-
-    for j in range(4):
-        right_root(j).wait_recv()
-
-    def right_mate_rows(m, carry):
-        total = jnp.zeros((256, 256), f32)
-        for q in range(NY):
-            total += jnp.dot(gc[q, m], rrv[1, pl.ds(256 * q, 256), :], preferred_element_type=f32)
-        tv[m] = total.astype(bf16)
-        return carry
-
-    lax.fori_loop(0, NX, right_mate_rows, 0)
-
-    def shipment(j):
-        return remote(
-            ship.at[:, quarters[j]], pv.at[pl.ds(base, 2), quarters[j]],
-            ship_send.at[j], ship_recv.at[j], (right_mate, s),
-        )
-
-    for i in range(2):
-        part = jnp.dot(rlv[i], tv[...].reshape(1024, 256), preferred_element_type=f32).astype(bf16)
-        ship[i] = part
-        norm += squares(part)
-    for j in range(4):
-        shipment(j).start()
-
-    norm = jnp.sum(norm, axis=1, keepdims=True)
-    lanes = lax.broadcasted_iota(jnp.int32, (8, 128), 1)
-    spot = jnp.where(lanes == inv[s], jnp.broadcast_to(norm, (8, 128)), 0.0)
-    norm_sum = SmallSum(small_p, sp_send, sp_recv, r, s)
-    norm_sum.start("y", spot)
-    norms[s] = norm_sum.finish("y")[:1]
-
-    def tell(i, carry):
-        ref = norms.at[s]
-        remote(ref, ref, norm_send, norm_recv, (r, lax.rem(s + i, NS))).start()
-        return carry
-
-    lax.fori_loop(1, NS, tell, 0)
-    for j in range(4):
-        arriving = pv.at[pl.ds(2 - base, 2), quarters[j]]
-        await_bytes(arriving, ship_recv.at[j])
-        give_back(2 - base, j)
-        give_back(3 - base, j)
 
     grads.drain()
     for j in range(4):
         left_root(j, side).wait_send()
         right_root(j).wait_send()
-        shipment(j).wait_send()
+        shipment(0, j).wait_send()
+        shipment(1, j).wait_send()
     sent = outb.at[pl.ds(0, NS - 1)]
     await_bytes(sent, bulk_send)
     await_bytes(sent, back_send)
@@ -455,11 +493,6 @@
 def per_device(
     grad, first_moment, second_moment, stat_left, stat_right, root_left, root_right, owner_slot
 ):
-    slots = jnp.arange(NS, dtype=jnp.int32)
-    numbers = jnp.arange(1, owner_slot.shape[0] + 1, dtype=jnp.int32)
-    inverse = jnp.sum(
-        jnp.where(owner_slot[None, :] == slots[:, None], numbers[None, :], 0), axis=1
-    ) - 1
     nblk, rows, cols = grad.shape
     span, width = stat_left.shape[1:]
     any_spec = pl.BlockSpec(memory_space=pl.ANY)
@@ -490,12 +523,17 @@
             pltpu.VMEM((NY, NX, width // NX, cols), bf16),
             pltpu.VMEM((NX, width // NX, cols), bf16),
             pltpu.VMEM((NX, width // NX, cols), bf16),
+            pltpu.VMEM((NX, width // NX, cols), bf16),
             pltpu.VMEM((2, width // NX, cols), bf16),
             pltpu.VMEM((nblk, 128), f32),
             pltpu.VMEM((SMALL, 8, 128), f32),
             pltpu.VMEM((SMALL, 8, 128), f32),
             pltpu.VMEM((NS, 1, 128), f32),
             pltpu.VMEM((8, 128), f32),
+            pltpu.VMEM((8, 128), jnp.int32),
+            pltpu.SMEM((8, 128), jnp.int32),
+            dma,
+            pltpu.SemaphoreType.REGULAR((10,)),
             dma((7,)),
             dma((5,)),
             dma,
@@ -506,7 +544,8 @@
             dma((2, NZ)),
             dma((NZ,)),
             dma((NZ,)),
-            *[dma((4,))] * 6,
+            *[dma((4,))] * 4,
+            *[dma((2, 4))] * 2,
             dma((4,)),
             dma((4,)),
             dma((4,)),
@@ -518,7 +557,7 @@
             collective_id=0, has_side_effects=True, vmem_limit_bytes=grant
         ),
     )(
-        inverse, grad, first_moment, second_moment, stat_left[0], stat_right[0],
+        owner_slot, grad, first_moment, second_moment, stat_left[0], stat_right[0],
         root_left[0], root_right[0],
     )
     update, first, second, left, right = pl.pallas_call(

time: 66.6 us -> 63.8 us (0.958)
  Pallas kernels: 64 us -> 63 us
    pallas_call x1, Pallas kernels: 60 us -> 59 us  [per_device(): pl.pallas_call(kernel, out_shape=(jax.ShapeDtypeStruct((NS, rows, cols),...]
where the time goes in v4:
time: 63.8 us; the launch traced here: 63.7 us
  Pallas kernels  63 us (99%)
  between operations  0.64 us (1%)
    pallas_call x1, Pallas kernels, per_device(): pl.pallas_call(kernel, out_shape=(jax.ShapeDtypeStruct((NS, rows, cols),...  59 us
    pallas_call x1, Pallas kernels, per_device(): pl.pallas_call(finish, out_shape=(jax.ShapeDtypeStruct(grad.shape, bf16),...  3.99 us

profile of v4, /device:TPU:1, one launch (start us, length us, event | category | flops | bytes accessed | tf_op | source)
XLA Modules:
  0.0 63.7 jit_solution(4303224910931083937)
XLA Ops:
  0.6 59.0 %shard_map.119 = (bf16[64,16,256]{2,1,0:T(8,128)(2,1)}, f32[8,128]{1,0:T(8,128)}, f32[48,16,256]{2,1,0:T(8,128)}, f32[48,16,256]{2,1,0:T(8,128)}, f32[256,1024]{1,0:T(8,128)}, /*index=5*/f32[256,1024]{1,0:T(8,128)}) custom-call(s32[48]{0:T(128)} %owner.3, bf16[48,16,256]{2,1,0:T(8,128)(2,1)} %grad.1, f32[48,16,256]{2,1,0:T(8,128)} %m1.1, f32[48,16,256]{2,1,0:T(8,128)} %m2.1, ...), custom_call_target="tpu_custom_call" | custom-call | tf_op jit(solution)/shard_map/pallas_call | solution.py:504
  59.7 4.0 %shard_map.120 = (bf16[48,16,256]{2,1,0:T(8,128)(2,1)}, f32[48,16,256]{2,1,0:T(8,128)}, f32[48,16,256]{2,1,0:T(8,128)}, f32[256,1024]{1,0:T(8,128)}, f32[256,1024]{1,0:T(8,128)}) custom-call(s32[48]{0:T(128)} %owner.3, bf16[64,16,256]{2,1,0:T(8,128)(2,1)} %get-tuple-element.16.returned, f32[8,128]{1,0:T(8,128)} %get-tuple-element.17.factor, ...), custom_call_target="tpu_custom_call" | custom-call | tf_op jit(solution)/shard_map/pallas_call | solution.py:563

commit v5 on v4

--- a/solution.py
+++ b/solution.py
@@ -21,7 +21,7 @@
 GROUP = NZ * NC
 Z_NEAR = (0, 1, 7, 2, 6, 3, 5, 4)
 Z_FAR = (2, 1, 3, 0)
-EARLY, FILL_LEFT, FILL_RIGHT, LAG = 3, 3, 4, 2
+LAG = 2
 
 
 def remote(src, dst, send_sem, recv_sem, device):
@@ -164,7 +164,8 @@
         return (r, there + lax.rem(c + other, NC))
 
     hellos = [(lax.rem(r + step, NY), s) for step in range(1, NY)]
-    hellos += [at(0, 0, 1), at(1, 0), at(-1, 0), at(0, 1), at(0, -1)]
+    hellos += [at(dx, 0, other) for dx in range(NX) for other in range(NC) if dx or other]
+    hellos += [at(0, 1), at(0, -1)]
     for device in hellos:
         pl.semaphore_signal(barrier, inc=1, device_id=device, device_id_type=MESH)
 
@@ -215,36 +216,9 @@
     near = [lax.rem(z + NZ - dz, NZ) for dz in Z_NEAR]
     grads = ColumnGather(gc, [rows_of(other, 32) for other in near], (g_os, g_or, g_fs, g_fr), r, s)
 
-    for j in range(FILL_RIGHT):
+    for j in range(4):
         right_root(j).start()
-        if j < FILL_LEFT:
-            left_root(j, side).start()
-
-    def say(i, device):
-        pl.semaphore_signal(word.at[i], inc=1, device_id=device, device_id_type=MESH)
-
-    def hear(i):
-        pl.semaphore_wait(word.at[i], 1)
-
-    say(0, at(1, 0))
-    say(1, at(-1, 0))
-    hear(0)
-    hear(1)
-    say(2, at(1, 0))
-    hear(2)
-    say(3, at(0, 1))
-    say(4, at(0, -1))
-    send_rows(0)
-    for step in range(1, 4):
-        hear(2 * step + 1)
-        hear(2 * step + 2)
-        say(2 * step + 3, at(0, 1))
-        if step < 3:
-            say(2 * step + 4, at(0, -1))
-        send_rows(step)
-        send_rows(NZ - step)
-    hear(9)
-    send_rows(4)
+        left_root(j, side).start()
 
     loads[3].wait()
     loads[4].wait()
@@ -261,7 +235,27 @@
         acc[pl.ds(b, 1), :] = jnp.sum(step, axis=0, keepdims=True)
         return carry
 
-    lax.fori_loop(0, nblk, adam, 0, unroll=2)
+    def say(i, device):
+        pl.semaphore_signal(word.at[i], inc=1, device_id=device, device_id_type=MESH)
+
+    def hear(i):
+        pl.semaphore_wait(word.at[i], 1)
+
+    say(0, at(0, 1))
+    say(1, at(0, -1))
+    send_rows(0)
+    for step in range(1, 4):
+        hear(2 * step - 2)
+        hear(2 * step - 1)
+        say(2 * step, at(0, 1))
+        if step < 3:
+            say(2 * step + 1, at(0, -1))
+        send_rows(step)
+        send_rows(NZ - step)
+        lax.fori_loop((step - 1) * nblk // 3, step * nblk // 3, adam, 0, unroll=2)
+    hear(6)
+    send_rows(4)
+
     store_first = pltpu.make_async_copy(m1v, first_out, out_sem.at[0])
     store_second = pltpu.make_async_copy(m2v, second_out, out_sem.at[1])
     store_first.start()
@@ -287,10 +281,6 @@
             adam_sum.start("y", adam_sum.finish("x"))
     for k in range(NZ - LAG, NZ):
         grads.pass_on(k)
-    for j in range(FILL_RIGHT, 4):
-        right_root(j).start()
-    for j in range(FILL_LEFT, 4):
-        left_root(j, side).start()
 
     def right_rows(k):
         parts = [gc[q, :, grads.rows[k], :].reshape(NX * 32, 256) for q in range(NY)]
@@ -358,49 +348,38 @@
         ).astype(bf16)
 
     def shipment(i, j):
-        plane = (r, left_mate)[i]
+        plane = base + i
         return remote(
             ship.at[i, quarters[j]], pv.at[plane, quarters[j]], ship_send.at[i, j],
             ship_recv.at[i, j], (right_mate, s),
         )
 
     def shipped(i, j):
-        plane = (right_mate, 3 - left_mate)[i]
+        plane = 2 - base + i
         await_bytes(pv.at[plane, quarters[j]], ship_recv.at[i, j])
         give_back(plane, j)
 
-    part = product(rlv[side], tv2)
-    ship[0] = part
     for j in range(4):
-        shipment(0, j).start()
-    norm = squares(part)
-    part = product(rlv[side], tv)
-    pv[r] = part
-    for j in range(4):
-        give_back(r, j)
-    norm += squares(part)
-
-    def mate_rows(pair):
-        for j in pair:
-            left_root(j, 1 - side).wait_recv()
-        left = jnp.concatenate([rlv[1 - side, quarters[j], :] for j in pair], axis=0)
-        away = product(left, tv2)
-        for n, j in enumerate(pair):
-            ship[1, quarters[j], :] = away[64 * n : 64 * n + 64]
-            shipment(1, j).start()
-        here = product(left, tv)
-        for n, j in enumerate(pair):
-            pv[left_mate, quarters[j], :] = here[64 * n : 64 * n + 64]
-            give_back(left_mate, j)
-        return squares(away) + squares(here)
-
-    norm += mate_rows((0, 1))
-    norm += mate_rows((2, 3))
+        left_root(j, 1 - side).wait_recv()
+    left = rlv[...].reshape(512, 1024)
+    part = product(left, tv2)
+    ship[0] = part[:256]
+    ship[1] = part[256:]
+    here = product(left, tv)
+    pv[base] = here[:256]
+    pv[base + 1] = here[256:]
+    norm = squares(part) + squares(here)
 
     norm = jnp.sum(norm, axis=1, keepdims=True)
     spot = jnp.where(lanes == inv[0, s], jnp.broadcast_to(norm, (8, 128)), 0.0)
     norm_sum = SmallSum(small_p, sp_send, sp_recv, r, s)
     norm_sum.start("y", spot)
+    for j in range(4):
+        shipment(0, j).start()
+        shipment(1, j).start()
+    for j in range(2):
+        give_back(base, j)
+        give_back(base + 1, j)
     norms[s] = norm_sum.finish("y")[:1]
 
     def tell(i, carry):
@@ -415,9 +394,11 @@
         return carry
 
     lax.fori_loop(0, NS, tell, 0, unroll=4)
+    for j in range(2, 4):
+        give_back(base, j)
+        give_back(base + 1, j)
     for j in range(4):
         shipped(0, j)
-    for j in range(4):
         shipped(1, j)
 
     loads[5].wait()
@@ -533,7 +514,7 @@
             pltpu.VMEM((8, 128), jnp.int32),
             pltpu.SMEM((8, 128), jnp.int32),
             dma,
-            pltpu.SemaphoreType.REGULAR((10,)),
+            pltpu.SemaphoreType.REGULAR((7,)),
             dma((7,)),
             dma((5,)),
             dma,

time: 63.8 us -> 62.1 us (0.973); the launches traced: 63.7 us -> 61.3 us
  Pallas kernels: 63 us -> 60.7 us
    pallas_call x1, Pallas kernels: 59 us -> 56.7 us  [per_device(): pl.pallas_call(kernel, out_shape=(jax.ShapeDtypeStruct((NS, rows, cols),...]
where the time goes in v5:
time: 62.1 us; the launch traced here: 61.3 us
  Pallas kernels  60.7 us (98%)
  between operations  0.64 us (1%)
    pallas_call x1, Pallas kernels, per_device(): pl.pallas_call(kernel, out_shape=(jax.ShapeDtypeStruct((NS, rows, cols),...  56.7 us
    pallas_call x1, Pallas kernels, per_device(): pl.pallas_call(finish, out_shape=(jax.ShapeDtypeStruct(grad.shape, bf16),...  3.99 us

profile of v5, /device:TPU:1, one launch (start us, length us, event | category | flops | bytes accessed | tf_op | source)
XLA Modules:
  0.0 61.3 jit_solution(9634495970965939919)
XLA Ops:
  0.6 56.7 %shard_map.119 = (bf16[64,16,256]{2,1,0:T(8,128)(2,1)}, f32[8,128]{1,0:T(8,128)}, f32[48,16,256]{2,1,0:T(8,128)}, f32[48,16,256]{2,1,0:T(8,128)}, f32[256,1024]{1,0:T(8,128)}, /*index=5*/f32[256,1024]{1,0:T(8,128)}) custom-call(s32[48]{0:T(128)} %owner.3, bf16[48,16,256]{2,1,0:T(8,128)(2,1)} %grad.1, f32[48,16,256]{2,1,0:T(8,128)} %m1.1, f32[48,16,256]{2,1,0:T(8,128)} %m2.1, ...), custom_call_target="tpu_custom_call" | custom-call | tf_op jit(solution)/shard_map/pallas_call | solution.py:485
  57.3 4.0 %shard_map.120 = (bf16[48,16,256]{2,1,0:T(8,128)(2,1)}, f32[48,16,256]{2,1,0:T(8,128)}, f32[48,16,256]{2,1,0:T(8,128)}, f32[256,1024]{1,0:T(8,128)}, f32[256,1024]{1,0:T(8,128)}) custom-call(s32[48]{0:T(128)} %owner.3, bf16[64,16,256]{2,1,0:T(8,128)(2,1)} %get-tuple-element.16.returned, f32[8,128]{1,0:T(8,128)} %get-tuple-element.17.factor, ...), custom_call_target="tpu_custom_call" | custom-call | tf_op jit(solution)/shard_map/pallas_call | solution.py:544

commit v6 on v5

--- a/solution.py
+++ b/solution.py
@@ -397,14 +397,17 @@
     for j in range(2, 4):
         give_back(base, j)
         give_back(base + 1, j)
-    for j in range(4):
+    for j in range(2):
         shipped(0, j)
         shipped(1, j)
-
     loads[5].wait()
     lax.fori_loop(0, 4, gram_left, 0)
     store_left = pltpu.make_async_copy(slv, left_out, out_sem.at[2])
     store_left.start()
+    for j in range(2, 4):
+        shipped(0, j)
+        shipped(1, j)
+
     loads[6].wait()
     lax.fori_loop(0, 4, gram_right, 0)
     store_right = pltpu.make_async_copy(srv, right_out, out_sem.at[3])
@@ -419,10 +422,6 @@
     sent = outb.at[pl.ds(0, NS - 1)]
     await_bytes(sent, bulk_send)
     await_bytes(sent, back_send)
-    store_first.wait()
-    store_second.wait()
-    store_left.wait()
-    store_right.wait()
     adam_sq = adam_sum.finish("y")
     others = norms.at[pl.ds(0, NS - 1)]
     await_bytes(others, norm_send)
@@ -432,6 +431,10 @@
     store_factor = pltpu.make_async_copy(facv, factor_out, out_sem.at[4])
     store_factor.start()
     await_bytes(returned, back_recv)
+    store_first.wait()
+    store_second.wait()
+    store_left.wait()
+    store_right.wait()
     store_factor.wait()
 
 

time: 62.1 us -> 62.1 us (level)
  no operation moved by 1% of the time
where the time goes in v6:
time: 62.1 us; the launch traced here: 61.3 us
  Pallas kernels  60.7 us (98%)
  between operations  0.64 us (1%)
    pallas_call x1, Pallas kernels, per_device(): pl.pallas_call(kernel, out_shape=(jax.ShapeDtypeStruct((NS, rows, cols),...  56.7 us
    pallas_call x1, Pallas kernels, per_device(): pl.pallas_call(finish, out_shape=(jax.ShapeDtypeStruct(grad.shape, bf16),...  3.99 us

profile of v6, /device:TPU:1, one launch (start us, length us, event | category | flops | bytes accessed | tf_op | source)
XLA Modules:
  0.0 61.3 jit_solution(5694003774460756438)
XLA Ops:
  0.6 56.7 %shard_map.119 = (bf16[64,16,256]{2,1,0:T(8,128)(2,1)}, f32[8,128]{1,0:T(8,128)}, f32[48,16,256]{2,1,0:T(8,128)}, f32[48,16,256]{2,1,0:T(8,128)}, f32[256,1024]{1,0:T(8,128)}, /*index=5*/f32[256,1024]{1,0:T(8,128)}) custom-call(s32[48]{0:T(128)} %owner.3, bf16[48,16,256]{2,1,0:T(8,128)(2,1)} %grad.1, f32[48,16,256]{2,1,0:T(8,128)} %m1.1, f32[48,16,256]{2,1,0:T(8,128)} %m2.1, ...), custom_call_target="tpu_custom_call" | custom-call | tf_op jit(solution)/shard_map/pallas_call | solution.py:488
  57.3 4.0 %shard_map.120 = (bf16[48,16,256]{2,1,0:T(8,128)(2,1)}, f32[48,16,256]{2,1,0:T(8,128)}, f32[48,16,256]{2,1,0:T(8,128)}, f32[256,1024]{1,0:T(8,128)}, f32[256,1024]{1,0:T(8,128)}) custom-call(s32[48]{0:T(128)} %owner.3, bf16[64,16,256]{2,1,0:T(8,128)(2,1)} %get-tuple-element.16.returned, f32[8,128]{1,0:T(8,128)} %get-tuple-element.17.factor, ...), custom_call_target="tpu_custom_call" | custom-call | tf_op jit(solution)/shard_map/pallas_call | solution.py:547
